TPU v7x, 32 devices: a whole 2x2x4 slice. The times are simulated.
32 devices in a mesh: rows: 4 (over y, x), seq: 8 (over z, core).
Axes of the slice: x: 2, y: 2, z: 4, core: 2. Of those that a mesh axis runs over, the one named last changes fastest.
Arguments:
- inputs: float32 [6, 4, 2048, 512], P(None, 'rows', 'seq'), may hold values from -6 to 6
- starts: int32 [6, 4, 3], P(None, 'rows'), may hold values from 0 to 2047, as said below
- first_gain: float32 [2, 512], replicated, may hold values from 0.1 to 1.9
- conv_taps: float32 [2, 512, 4], replicated, may hold values from -3 to 3
- in_weight: float32 [2, 512, 2048], replicated, may hold values from -0.25 to 0.25
- gate_bias: float32 [2, 1024], replicated, may hold values from -8 to 0
- out_weight: float32 [2, 1024, 512], replicated, may hold values from -0.375 to 0.375
- second_gain: float32 [2, 512], replicated, may hold values from 0.1 to 1.9
- up_weight: float32 [2, 512, 2048], replicated, may hold values from -0.25 to 0.25
- down_weight: float32 [2, 2048, 512], replicated, may hold values from -0.125 to 0.125
- cotangent: float32 [6, 4, 2048, 512], P(None, 'rows', 'seq'), may hold values from -6 to 6
Outputs:
- outputs: float32 [6, 4, 2048, 512], P(None, 'rows', 'seq')
- input_grad: float32 [6, 4, 2048, 512], P(None, 'rows', 'seq')
- first_grad: float32 [2, 512], replicated
- taps_grad: float32 [2, 512, 4], replicated
- in_grad: float32 [2, 512, 2048], P(None, 'seq', 'rows')
- bias_grad: float32 [2, 1024], replicated
- out_grad: float32 [2, 1024, 512], P(None, 'seq', 'rows')
- second_grad: float32 [2, 512], replicated
- up_grad: float32 [2, 512, 2048], P(None, 'seq', 'rows')
- down_grad: float32 [2, 2048, 512], P(None, 'seq', 'rows')
Inputs may be any that keep to these rules, and one draw needn't show every extreme that they name: `starts`: each row lists 3 increasing offsets: the first is 0, the second lies in the row's first 256 positions, the third in its last 256 positions.
All inputs are finite; a program needn't handle non-finite values.
Results may differ from a plain program's by a relative error of at most 0.0003.
Values sent between devices are 32-bit elements; how exact they have to be, the bound alone decides.
No kernel may reach another device: no remote copies, remote signals or barrier semaphores. Data moves between devices by JAX's collectives and lax.ppermute only.
A program may use at most 384 MiB of HBM per device.

v0:
```python
import jax
import jax.numpy as jnp
from jax import lax
from jax.sharding import PartitionSpec as P

epsilon = 1e-05


def from_behind(block, axis, distance):
    devices = range(lax.axis_size(axis))
    route = [(i - distance, i) for i in devices if i - distance in devices]
    return lax.ppermute(block, axis, route)


def rms_scale(values, gain):
    return values * lax.rsqrt(jnp.mean(values * values, -1, keepdims=True) + epsilon) * gain


def combine_pairs(earlier, later):
    return (earlier[0] * later[0], later[0] * earlier[1] + later[1])


def gelu_tanh(values):
    return jax.nn.gelu(values, approximate=True)


def gate_values(logit, candidate, bias, keep):
    shifted = logit + bias
    return (jax.nn.sigmoid(-shifted) * keep, jax.nn.sigmoid(shifted) * jax.nn.softplus(candidate))


def project(left, right):
    return jnp.einsum("bck,kj->bcj", left, right, precision=lax.Precision.HIGHEST)


def project_back(left, right):
    return jnp.einsum("bck,jk->bcj", left, right, precision=lax.Precision.HIGHEST)


def weight_grad(left, right):
    return jnp.einsum("bci,bcj->ij", left, right, precision=lax.Precision.HIGHEST)


def document_masks(starts_rows, group, taps):
    offset = lax.axis_index("seq") * group
    positions = offset + jnp.arange(1 - taps, group + taps - 1, dtype=jnp.int32)
    doc_ext = jnp.sum((starts_rows[:, None, :] <= positions[None, :, None]).astype(jnp.int32), -1)
    own = doc_ext[:, taps - 1 : taps - 1 + group]
    keep = (own == doc_ext[:, taps - 2 : taps - 2 + group]).astype(jnp.float32)[:, :, None]
    masks = [
        (doc_ext[:, taps - 1 - j : taps - 1 - j + group] == own).astype(jnp.float32)[:, :, None]
        for j in range(taps)
    ]
    ahead = [
        (doc_ext[:, taps - 1 + j : taps - 1 + j + group] == own).astype(jnp.float32)[:, :, None]
        for j in range(taps)
    ]
    return (keep, masks, ahead)


def forward_carry(total, local_end):

    def relay_step(step, incoming):
        return from_behind(local_end + total * incoming, "seq", 1)

    return lax.fori_loop(0, lax.axis_size("seq") - 1, relay_step, jnp.zeros_like(local_end))


def backward_carry(total, local_start):

    def relay_back(step, incoming):
        return from_behind(local_start + total * incoming, "seq", -1)

    return lax.fori_loop(0, lax.axis_size("seq") - 1, relay_back, jnp.zeros_like(local_start))


def layer_forward(values, weights, keep, masks):
    gain_first, taps_weight, weight_in, bias, weight_out, gain_second, weight_up, weight_down = (
        weights
    )
    taps = taps_weight.shape[1]
    group = values.shape[1]
    hidden = weight_out.shape[0]
    normed = rms_scale(values, gain_first)
    edge = from_behind(normed[:, group - taps + 1 :], "seq", 1)
    extended = jnp.concatenate([edge, normed], 1)
    mixed = taps_weight[:, 0] * masks[0] * extended[:, taps - 1 : taps - 1 + group]
    for j in range(1, taps):
        mixed = (
            mixed + taps_weight[:, j] * masks[j] * extended[:, taps - 1 - j : taps - 1 - j + group]
        )
    projected = project(mixed, weight_in)
    logit = projected[:, :, :hidden]
    candidate = projected[:, :, hidden:]
    decay, drive = gate_values(logit, candidate, bias, keep)
    total, local = lax.associative_scan(combine_pairs, (decay, drive), axis=1)
    incoming = forward_carry(total[:, -1], local[:, -1])
    states = local + total * incoming[:, None]
    middle = values + project(states, weight_out)
    normed2 = rms_scale(middle, gain_second)
    pre = project(normed2, weight_up)
    act = gelu_tanh(pre)
    result = middle + project(act, weight_down)
    return (
        result,
        (
            values,
            extended,
            mixed,
            logit,
            candidate,
            decay,
            incoming,
            states,
            middle,
            normed2,
            pre,
            act,
        ),
    )


def layer_backward(grad_out, weights, saved, keep, masks, ahead):
    gain_first, taps_weight, weight_in, bias, weight_out, gain_second, weight_up, weight_down = (
        weights
    )
    (
        values,
        extended,
        mixed,
        logit,
        candidate,
        decay,
        incoming,
        states,
        middle,
        normed2,
        pre,
        act,
    ) = saved
    taps = taps_weight.shape[1]
    group = values.shape[1]
    down_g = weight_grad(act, grad_out)
    act_grad = project_back(grad_out, weight_down)
    pre_grad = jax.vjp(gelu_tanh, pre)[1](act_grad)[0]
    up_g = weight_grad(normed2, pre_grad)
    normed2_grad = project_back(pre_grad, weight_up)
    middle_part, second_g = jax.vjp(rms_scale, middle, gain_second)[1](normed2_grad)
    middle_grad = grad_out + middle_part
    out_g = weight_grad(states, middle_grad)
    state_grad = project_back(middle_grad, weight_out)
    following = jnp.concatenate([decay[:, 1:], jnp.ones_like(decay[:, :1])], 1)
    reach, local_adj = lax.associative_scan(
        combine_pairs, (following, state_grad), axis=1, reverse=True
    )
    returning = backward_carry(decay[:, 0] * reach[:, 0], decay[:, 0] * local_adj[:, 0])
    adjoint = local_adj + reach * returning[:, None]
    previous = jnp.concatenate([incoming[:, None], states[:, :-1]], 1)

    def gate_only(logit_part, cand_part, bias_part):
        return gate_values(logit_part, cand_part, bias_part, keep)

    logit_grad, cand_grad, bias_g = jax.vjp(gate_only, logit, candidate, bias)[1](
        (adjoint * previous, adjoint)
    )
    projected_grad = jnp.concatenate([logit_grad, cand_grad], -1)
    in_g = weight_grad(mixed, projected_grad)
    mixed_grad = project_back(projected_grad, weight_in)
    tap_list = []
    for j in range(taps):
        tap_list.append(
            jnp.sum(
                masks[j] * mixed_grad * extended[:, taps - 1 - j : taps - 1 - j + group], (0, 1)
            )
        )
    taps_g = jnp.stack(tap_list, -1)
    padded_grad = jnp.concatenate([mixed_grad, jnp.zeros_like(mixed_grad[:, : taps - 1])], 1)
    normed_grad = taps_weight[:, 0] * ahead[0] * mixed_grad
    for j in range(1, taps):
        normed_grad = normed_grad + taps_weight[:, j] * ahead[j] * padded_grad[:, j : j + group]
    head_grad = mixed_grad[:, : taps - 1]
    edge_rows = jnp.zeros_like(head_grad)
    for j in range(1, taps):
        term = taps_weight[:, j] * masks[j][:, :j] * head_grad[:, :j]
        edge_rows = edge_rows + jnp.pad(term, ((0, 0), (taps - 1 - j, 0), (0, 0)))
    edge_back = from_behind(edge_rows, "seq", -1)
    normed_grad = normed_grad.at[:, group - taps + 1 :].add(edge_back)
    values_grad, first_g = jax.vjp(rms_scale, values, gain_first)[1](normed_grad)
    return (
        middle_grad + values_grad,
        (first_g, taps_g, in_g, bias_g, out_g, second_g, up_g, down_g),
    )


def per_device(
    inputs,
    starts,
    first_gain,
    conv_taps,
    in_weight,
    gate_bias,
    out_weight,
    second_gain,
    up_weight,
    down_weight,
    cotangent,
):
    shape = inputs.shape
    batch = shape[0] * shape[1]
    group = shape[2]
    width = shape[3]
    taps = conv_taps.shape[2]
    layers = in_weight.shape[0]
    keep, masks, ahead = document_masks(starts.reshape(batch, -1), group, taps)
    params = (
        first_gain,
        conv_taps,
        in_weight,
        gate_bias,
        out_weight,
        second_gain,
        up_weight,
        down_weight,
    )
    current = inputs.reshape(batch, group, width)
    stored = []
    for layer in range(layers):
        weights = tuple((param[layer] for param in params))
        current, saved = layer_forward(current, weights, keep, masks)
        stored.append((weights, saved))
    grad_now = cotangent.reshape(batch, group, width)
    collected = [None] * layers
    for layer in reversed(range(layers)):
        grad_now, collected[layer] = layer_backward(
            grad_now, stored[layer][0], stored[layer][1], keep, masks, ahead
        )
    stacked = [
        jnp.stack([collected[layer][index] for layer in range(layers)]) for index in range(8)
    ]
    large = (stacked[2], stacked[4], stacked[6], stacked[7])
    partial_sums = (
        lax.psum_scatter(large[0], "seq", scatter_dimension=1, tiled=True),
        lax.psum_scatter(large[1], "seq", scatter_dimension=1, tiled=True),
        lax.psum_scatter(large[2], "seq", scatter_dimension=1, tiled=True),
        lax.psum_scatter(large[3], "seq", scatter_dimension=1, tiled=True),
    )
    large = (
        lax.psum_scatter(partial_sums[0], "rows", scatter_dimension=2, tiled=True),
        lax.psum_scatter(partial_sums[1], "rows", scatter_dimension=2, tiled=True),
        lax.psum_scatter(partial_sums[2], "rows", scatter_dimension=2, tiled=True),
        lax.psum_scatter(partial_sums[3], "rows", scatter_dimension=2, tiled=True),
    )
    small = lax.psum((stacked[0], stacked[1], stacked[3], stacked[5]), ("rows", "seq"))
    return (
        current.reshape(shape),
        grad_now.reshape(shape),
        small[0],
        small[1],
        large[0],
        small[2],
        large[1],
        small[3],
        large[2],
        large[3],
    )


def solution(mesh):
    in_specs = (
        P(None, "rows", "seq", None),
        P(None, "rows", None),
        P(),
        P(),
        P(),
        P(),
        P(),
        P(),
        P(),
        P(),
        P(None, "rows", "seq", None),
    )
    out_specs = (
        P(None, "rows", "seq", None),
        P(None, "rows", "seq", None),
        P(),
        P(),
        P(None, "seq", "rows"),
        P(),
        P(None, "seq", "rows"),
        P(),
        P(None, "seq", "rows"),
        P(None, "seq", "rows"),
    )
    return jax.shard_map(
        per_device, mesh=mesh, in_specs=in_specs, out_specs=out_specs, check_vma=False
    )
```

profile of v0, /device:TPU:0, one launch (start us, length us, event | category | flops | bytes accessed | tf_op | source)
XLA Modules:
  0.0 2811.2 jit_solution(2984684313350893925)
XLA Ops:
  27.0 24.6 fusion.54
  62.5 14.4 slice.1328
  270.8 14.4 slice.1271
  500.0 34.6 %while.42 = (s32[]{:T(128)}, f32[6,1024]{1,0:T(8,128)S(1)}, f32[6,1024]{1,0:T(8,128)S(1)}, f32[6,1024]{1,0:T(8,128)S(1)}, s32[]{:T(128)}) while((s32[]{:T(128)}, f32[6,1024]{1,0:T(8,128)S(1)}, f32[6,1024]{1,0:T(8,128)S(1)}, f32[6,1024]{1,0:T(8,128)S(1)}, s32[]{:T(128)}) %tuple.239), condition=%wide.region_3.4_spmd, body=%wide.region_2.3_spmd.sunk | while | flops 12290 | bytes 196709 | solution.py:66
  555.9 22.7 fusion.51
  578.6 33.4 %multiply_reduce_fusion.16 = (f32[6,256]{1,0:T(8,128)S(1)}, f32[6,256,512]{2,1,0:T(8,128)S(1)}) fusion(f32[6,256,512]{2,1,0:T(8,128)S(1)} %get-tuple-element.394, f32[2,2048,512]{2,1,0:T(8,128)} %param.33, f32[6,256,2048]{2,1,0:T(8,128)S(1)} %fusion.51), kind=kOutput, calls=%fused_computation.181 | convolution fusion | flops 19354875904 | bytes 23074816 | tf_op jit(solution)/shard_map/bck,kj->bcj/dot_general | solution.py:33
  621.3 24.6 fusion.44
  656.8 14.4 slice.1422
  801.2 14.4 slice.1365
  943.2 36.8 %while.43 = (s32[]{:T(128)}, f32[6,1024]{1,0:T(8,128)S(1)}, f32[6,1024]{1,0:T(8,128)S(1)}, f32[6,1024]{1,0:T(8,128)S(1)}, s32[]{:T(128)}) while((s32[]{:T(128)}, f32[6,1024]{1,0:T(8,128)S(1)}, f32[6,1024]{1,0:T(8,128)S(1)}, f32[6,1024]{1,0:T(8,128)S(1)}, s32[]{:T(128)}) %tuple.240), condition=%wide.region_7.8_spmd, body=%wide.region_6.7_spmd.sunk | while | flops 12290 | bytes 196709 | solution.py:66
  1053.5 24.9 fusion.41
  1078.4 33.0 %fusion.11 = f32[6,256,2048]{2,1,0:T(8,128)} fusion(f32[6,256,2048]{2,1,0:T(8,128)S(1)} %fusion.41, f32[2,2048,512]{2,1,0:T(8,128)} %param.33, f32[6,1,256,512]{3,2,1,0:T(8,128)S(1)} %copy-done.103), kind=kOutput, calls=%fused_computation.25 | convolution fusion | flops 19387121664 | bytes 32505856 | tf_op jit(solution)/shard_map/bck,jk->bcj/dot_general | solution.py:37
  1111.4 25.4 multiply_reduce_fusion
  1208.8 24.8 slice.1456
  1233.6 15.6 slice.1449
  1249.3 24.8 slice.1451
  1274.0 15.7 slice.1453
  1377.3 15.9 slice.1447
  1393.2 24.9 slice.1509
  1554.9 48.5 %rev.16 = f32[6,256,1024]{2,1,0:T(8,128)} reverse(f32[6,256,1024]{2,1,0:T(8,128)} %add.1051), dimensions={1} | reverse | bytes 12582912 | tf_op jit(solution)/shard_map/rev | solution.py:153
  1603.3 48.5 %rev.17 = f32[6,256,1024]{2,1,0:T(8,128)} reverse(f32[6,256,1024]{2,1,0:T(8,128)} %add.1059), dimensions={1} | reverse | bytes 12582912 | tf_op jit(solution)/shard_map/rev | solution.py:153
  1651.8 37.1 %while.44 = (s32[]{:T(128)}, f32[6,1024]{1,0:T(8,128)S(1)}, f32[6,1024]{1,0:T(8,128)S(1)}, f32[6,1024]{1,0:T(8,128)S(1)}, s32[]{:T(128)}) while((s32[]{:T(128)}, f32[6,1024]{1,0:T(8,128)S(1)}, f32[6,1024]{1,0:T(8,128)S(1)}, f32[6,1024]{1,0:T(8,128)S(1)}, s32[]{:T(128)}) %tuple.241), condition=%wide.region_11.12_spmd, body=%wide.region_10.11_spmd.sunk | while | flops 12290 | bytes 196709 | solution.py:74
  1689.0 15.4 fusion.205
  1704.4 26.3 fusion.15
  1742.6 33.0 %fusion.5 = f32[6,256,2048]{2,1,0:T(8,128)S(1)} fusion(f32[6,256,2048]{2,1,0:T(8,128)} %copy-done.63, f32[6,256,512]{2,1,0:T(8,128)S(1)} %fusion.77, f32[2,2048,512]{2,1,0:T(8,128)} %param.33), kind=kOutput, calls=%fused_computation.19 | convolution fusion | flops 19387121664 | bytes 32505856 | tf_op jit(solution)/shard_map/bck,jk->bcj/dot_general | solution.py:37
  1775.7 25.2 multiply_reduce_fusion.1
  1814.6 27.8 fusion.68
  1842.5 26.3 fusion.69
  1875.1 24.3 convolution_bitcast_fusion
  1899.4 24.4 convolution_bitcast_fusion.1
  1976.3 15.7 slice.1552
  1992.0 24.8 slice.1543
  2016.8 24.8 slice.1545
  2041.6 25.0 fusion.70
  2121.1 24.7 slice.1547
  2145.8 15.8 slice.1549
  2249.5 15.9 slice.1605
  2382.3 48.5 %rev.18 = f32[6,256,1024]{2,1,0:T(8,128)} reverse(f32[6,256,1024]{2,1,0:T(8,128)} %add.1091), dimensions={1} | reverse | bytes 12582912 | tf_op jit(solution)/shard_map/rev | solution.py:153
  2461.0 48.4 %rev.19 = f32[6,256,1024]{2,1,0:T(8,128)} reverse(f32[6,256,1024]{2,1,0:T(8,128)} %add.1099), dimensions={1} | reverse | bytes 12582912 | tf_op jit(solution)/shard_map/rev | solution.py:153
  2510.9 37.3 %while.45 = (s32[]{:T(128)}, f32[6,1024]{1,0:T(8,128)S(1)}, f32[6,1024]{1,0:T(8,128)S(1)}, f32[6,1024]{1,0:T(8,128)S(1)}, s32[]{:T(128)}) while((s32[]{:T(128)}, f32[6,1024]{1,0:T(8,128)S(1)}, f32[6,1024]{1,0:T(8,128)S(1)}, f32[6,1024]{1,0:T(8,128)S(1)}, s32[]{:T(128)}) %tuple.238), condition=%wide.region_15.0_spmd, body=%wide.region_14.0_spmd.sunk | while | flops 12290 | bytes 196709 | solution.py:74
  2548.2 15.4 fusion.203
  2566.2 20.5 fusion.71
  2593.0 28.2 %add_bitcast_fusion = f32[6,1,256,512]{3,2,1,0:T(8,128)} fusion(f32[6,256,512]{2,1,0:T(8,128)S(1)} %copy-done.10, f32[2,2048,512]{2,1,0:T(8,128)} %param.33, f32[6,256,2048]{2,1,0:T(8,128)} %copy-done.62), kind=kOutput, calls=%fused_computation.177 | convolution fusion | flops 19353305088 | bytes 23068672 | tf_op jit(solution)/shard_map/bck,kj->bcj/dot_general | solution.py:33
  2621.4 33.7 %multiply_reduce_fusion.4 = (f32[512]{0:T(512)S(1)}, f32[512]{0:T(512)S(1)}, f32[512]{0:T(512)S(1)}, f32[512]{0:T(512)S(1)}, f32[512]{0:T(512)S(1)}, /*index=5*/...) fusion(f32[6,256,512]{2,1,0:T(8,128)} %copy-done.86, f32[6,256]{1,0:T(8,128)S(1)} %copy-done.137, ...), kind=kOutput, calls=%fused_computation.162 | convolution fusion | flops 19352514560 | bytes 29468672 | tf_op jit(solution)/shard_map/bck,jk->bcj/dot_general | solution.py:37
  2658.3 25.5 reduce-scatter.9.cloned.1.call-done
  2697.3 38.7 %all-reduce.138 = (f32[2,512]{1,0:T(2,128)}, f32[2,512,4]{1,2,0:T(4,128)}, f32[2,1024]{1,0:T(2,128)}, f32[2,512]{1,0:T(2,128)}) all-reduce(f32[2,512]{1,0:T(2,128)S(1)} %pad_maximum_fusion.72, f32[2,512,4]{1,2,0:T(4,128)S(1)} %pad_maximum_fusion.70, ...), channel_id=1, replica_groups=mesh['rows'=4,'seq'=8] {'rows','seq'}, use_global_device_ids=true, to_apply=%region_19.21 | all-reduce | flops 8192 | bytes 65536 | tf_op jit(solution)/shard_map/psum | solution.py:253
  2741.3 31.2 %reduce-scatter.19.cloned.1.call-done = f32[2,64,512]{2,1,0:T(8,128)} async-done(((f32[2,64,2048]{2,1,0:T(8,128)}), f32[2,64,512]{2,1,0:T(8,128)}) %reduce-scatter.19.cloned.1.call-update) | async-done | bytes 262160 | tf_op jit(solution)/shard_map/reduce_scatter | solution.py:250
  2772.5 31.5 %reduce-scatter.11.cloned.1.call-done = f32[2,64,512]{2,1,0:T(8,128)} async-done(((f32[2,64,2048]{2,1,0:T(8,128)}), f32[2,64,512]{2,1,0:T(8,128)}) %reduce-scatter.11.cloned.1.call-update) | async-done | bytes 262160 | tf_op jit(solution)/shard_map/reduce_scatter | solution.py:248
  (1193 shorter events, 1656.7 us)
Async XLA Ops:
  7.2 2584.0 %reduce-scatter.13.cloned.1.call-start = ((), (), s32[]{:S(2)}) async-start(), calls=%async_computation.10 | async-start | bytes 4718592 | tf_op jit(solution)/shard_map/reduce_scatter | solution.py:243
  13.5 6.2 collective-permute-start.4
  17.9 601.1 %copy-start.130 = (f32[6,256]{1,0:T(8,128)}, f32[6,256]{1,0:T(8,128)S(1)}, u32[]{:S(2)}) copy-start(f32[6,256]{1,0:T(8,128)S(1)} %get-tuple-element.375) | copy-start | bytes 18436
  17.9 628.0 %copy-start.123 = (f32[6,256]{1,0:T(8,128)}, f32[6,256]{1,0:T(8,128)S(1)}, u32[]{:S(2)}) copy-start(f32[6,256]{1,0:T(8,128)S(1)} %get-tuple-element.377) | copy-start | bytes 18436
  500.0 5.4 collective-permute-start
  505.5 3.1 collective-permute-start
  508.6 5.1 collective-permute-start
  513.7 5.2 collective-permute-start
  518.9 5.2 collective-permute-start
  524.1 5.2 collective-permute-start
  529.4 5.2 collective-permute-start
  613.7 5.2 collective-permute-start.5
  943.2 5.4 collective-permute-start.1
  948.6 5.2 collective-permute-start.1
  953.8 5.2 collective-permute-start.1
  959.1 5.2 collective-permute-start.1
  964.3 5.2 collective-permute-start.1
  969.5 5.2 collective-permute-start.1
  974.8 5.2 collective-permute-start.1
  1053.4 86.9 %slice-start.4 = ((s8[6291456]{0:T(1024)(128)(4,1)}), s8[4194304]{0:T(1024)(128)(4,1)S(1)}, s32[]{:S(2)}) async-start(s8[6291456]{0:T(1024)(128)(4,1)} %bitcast.248), calls=%async_computation.20 | async-start | bytes 8388608
  1603.3 85.7 %copy-start.138 = (f32[6,1,1024]{2,1,0:T(1,128)S(1)}, f32[6,1,1024]{2,1,0:T(1,128)}, u32[]{:S(2)}) copy-start(f32[6,1,1024]{2,1,0:T(1,128)} %broadcast_in_dim.19) | copy-start | bytes 73732
  1603.3 85.7 %copy-start.201 = (f32[1,1024]{1,0:T(1,128)S(1)}, f32[1,1024]{1,0:T(1,128)}, u32[]{:S(2)}) copy-start(f32[1,1024]{1,0:T(1,128)} %get-tuple-element.383) | copy-start | bytes 12292
  1651.9 5.1 collective-permute-start.2
  1657.0 5.8 collective-permute-start.2
  1662.8 5.2 collective-permute-start.2
  1668.0 5.2 collective-permute-start.2
  1673.3 5.2 collective-permute-start.2
  1678.5 5.2 collective-permute-start.2
  1683.7 5.2 collective-permute-start.2
  1731.1 5.3 collective-permute-start.6
  1814.6 777.2 %reduce-scatter.21.cloned.1.call-start = ((), (), s32[]{:S(2)}) async-start(), calls=%async_computation.14 | async-start | bytes 9437184 | tf_op jit(solution)/shard_map/reduce_scatter | solution.py:245
  1873.2 747.9 %reduce-scatter.17.cloned.1.call-start = ((), (), s32[]{:S(2)}) async-start(), calls=%async_computation.12 | async-start | bytes 9437184 | tf_op jit(solution)/shard_map/reduce_scatter | solution.py:244
  1927.6 756.2 %reduce-scatter.9.cloned.1.call-start = ((), (), s32[]{:S(2)}) async-start(), calls=%async_computation.8 | async-start | bytes 9437184 | tf_op jit(solution)/shard_map/reduce_scatter | solution.py:242
  2461.0 87.1 %copy-start.125 = (f32[6,256]{1,0:T(8,128)S(1)}, f32[6,256]{1,0:T(8,128)}, u32[]{:S(2)}) copy-start(f32[6,256]{1,0:T(8,128)} %copy-done.123) | copy-start | bytes 18436
  2461.0 87.1 %copy-start.139 = (f32[6,1,1024]{2,1,0:T(1,128)S(1)}, f32[6,1,1024]{2,1,0:T(1,128)}, u32[]{:S(2)}) copy-start(f32[6,1,1024]{2,1,0:T(1,128)} %broadcast_in_dim.25) | copy-start | bytes 73732
  2461.0 87.1 %copy-start.199 = (f32[1,1024]{1,0:T(1,128)S(1)}, f32[1,1024]{1,0:T(1,128)}, u32[]{:S(2)}) copy-start(f32[1,1024]{1,0:T(1,128)} %copy-done.198) | copy-start | bytes 12292
  2510.9 5.6 collective-permute-start.3
  2516.5 5.4 collective-permute-start.3
  2522.0 5.2 collective-permute-start.3
  2527.2 5.2 collective-permute-start.3
  2532.5 5.2 collective-permute-start.3
  2537.7 5.2 collective-permute-start.3
  2542.9 5.2 collective-permute-start.3
  2591.1 149.4 %reduce-scatter.15.cloned.1.call-start = ((), (), s32[]{:S(2)}) async-start(), calls=%async_computation.11 | async-start | bytes 655360 | tf_op jit(solution)/shard_map/reduce_scatter | solution.py:249
  2591.7 149.6 %reduce-scatter.23.cloned.1.call-start = ((), (), s32[]{:S(2)}) async-start(), calls=%async_computation.15 | async-start | bytes 1310720 | tf_op jit(solution)/shard_map/reduce_scatter | solution.py:251
  2592.3 180.2 %reduce-scatter.19.cloned.1.call-start = ((), (), s32[]{:S(2)}) async-start(), calls=%async_computation.13 | async-start | bytes 1310720 | tf_op jit(solution)/shard_map/reduce_scatter | solution.py:250
  2621.3 182.7 %reduce-scatter.11.cloned.1.call-start = ((), (), s32[]{:S(2)}) async-start(), calls=%async_computation.9 | async-start | bytes 1310720 | tf_op jit(solution)/shard_map/reduce_scatter | solution.py:248
  2656.9 34.4 %collective-permute-start.7 = (f32[6,3,512]{2,1,0:T(4,128)S(1)}, f32[6,3,512]{2,1,0:T(4,128)S(1)}, u32[]{:S(2)}, u32[]{:S(2)}) collective-permute-start(f32[6,3,512]{2,1,0:T(4,128)S(1)} %fusion.154), channel_id=1, source_target_pairs={{1,0},{2,1},{3,2},{4,3},{5,4},{6,5},{7,6},{9,8},{10,9},{11,10},{12... | collective-permute-start | bytes 110600 | tf_op jit(solution)/shard_map/ppermute | solution.py:12
  (240 other events, 3239.1 us)
Sparse Core Ops, SparseCore 0:
  1814.7 54.3 reduce-scatter.12
  1873.3 94.0 reduce-scatter.20
  1969.7 87.9 reduce-scatter.16
  2591.2 92.5 reduce-scatter.8
  2687.0 22.9 reduce-scatter.14
  2713.6 27.6 reduce-scatter.22
  2744.8 27.7 reduce-scatter.18
  2776.3 27.7 reduce-scatter.10
where the time goes:
time: 2870 us; the launch traced here: 2810 us
  local copies, waits for them, and re-layouts  1560 us (54%)
  matrix products  550 us (19%)
  other arithmetic  397 us (14%)
  waiting for transfers between devices  160 us (6%)
  starting transfers between devices  87.1 us (3%)
  blocking collectives  38.7 us (1%)
    slice x114, local copies, waits for them, and re-layouts, layer_backward(): lax.associative_scan(combine_pairs, (following, state_grad), axis=1, reve...  552 us
    slice x104, local copies, waits for them, and re-layouts, layer_forward(): total, local = lax.associative_scan(combine_pairs, (decay, drive), axis=1)  342 us
    pad x56, local copies, waits for them, and re-layouts, layer_forward(): total, local = lax.associative_scan(combine_pairs, (decay, drive), axis=1)  231 us
    dot_general x8, matrix products, project_back(): jnp.einsum('bck,jk->bcj', left, right, precision=lax.Precision.HIGHEST)  199 us
    rev x4, local copies, waits for them, and re-layouts, layer_backward(): lax.associative_scan(combine_pairs, (following, state_grad), axis=1, reve...  194 us
    dot_general x8, matrix products, project(): jnp.einsum('bck,kj->bcj', left, right, precision=lax.Precision.HIGHEST)  182 us
    pad x56, local copies, waits for them, and re-layouts, layer_backward(): lax.associative_scan(combine_pairs, (following, state_grad), axis=1, reve...  171 us
    dot_general x8, matrix products, weight_grad(): jnp.einsum('bci,bcj->ij', left, right, precision=lax.Precision.HIGHEST)  170 us
  transfers between devices with their start and end apart: 40, of which 34 were waited for; matrix products, arithmetic and copies ran while one was open for 29% of the time, Pallas kernels for 0%

commit v1 on v0

v1 whole, which is shorter than its diff:
```python
import functools
import math

import jax
import jax.numpy as jnp
from jax import lax
from jax.experimental import pallas as pl
from jax.experimental.pallas import tpu as pltpu
from jax.sharding import PartitionSpec as P

epsilon = 1e-05
C0 = math.sqrt(2.0 / math.pi)
C1 = C0 * 0.044715
NN = (((1,), (0,)), ((), ()))
NT = (((1,), (1,)), ((), ()))
BF = jnp.bfloat16
F32 = jnp.float32
VMEM = 60 * 1024 * 1024
CHUNK = 512
HALF = 256
LARGE = 256 * 1024


def split(v):
    high = v.astype(BF)
    return high, (v - high.astype(F32)).astype(BF)


def dot(left, right, dims=NN):
    return lax.dot_general(left, right, dimension_numbers=dims, preferred_element_type=F32)


def put_right(ref, high, low, axis, at=0):
    size = ref.shape[axis] // 3
    count = high.shape[axis]
    for k, part in enumerate((high, high, low)):
        where = pl.ds(k * size + at, count)
        if axis == 0:
            ref[where, :] = part
        else:
            ref[:, where] = part


def put_left(ref, v, rows):
    high, low = split(v)
    size = ref.shape[1] // 3
    for k, part in enumerate((high, low, high)):
        ref[rows, k * size : (k + 1) * size] = part


def put_left_turned(ref, v, cols):
    size = ref.shape[1] // 3
    for k in range(0, v.shape[1], 128):
        high, low = split(v[:, k : k + 128].T)
        for q, part in enumerate((high, low, high)):
            ref[k : k + 128, pl.ds(q * size + cols, part.shape[1])] = part


def turn_slice(cat_ref, b, size, n, high_ref, low_ref):
    width = cat_ref.shape[1] // 3
    count = high_ref.shape[0]
    rows = slice(b * size, (b + 1) * size)
    for q, ref in enumerate((high_ref, low_ref)):
        part = cat_ref[rows, pl.ds(pl.multiple_of(q * width + n * count, 128), count)]
        ref[:, rows] = part.T


def three_left(high_ref, low_ref):
    return jnp.concatenate([high_ref[...], low_ref[...], high_ref[...]], 1)


def load_rows(ref, b, tmp, put):
    size = ref.shape[1]
    if tmp is not None:
        for k in range(tmp.shape[0]):
            tmp[k] = ref[b, :, 128 * k : 128 * (k + 1)]
    for r in range(0, size, 16):
        if tmp is None:
            put(r, ref[b, r : r + 16, :])
        else:
            groups = [
                jnp.concatenate([tmp[k, pl.ds(i, 8, stride=size // 8), :] for k in range(tmp.shape[0])], 1)
                for i in (r // 8, r // 8 + 1)
            ]
            put(r, jnp.concatenate(groups, 0))


def store_rows(ref, b, values, tmp):
    if tmp is None:
        ref[b] = values
        return
    rows = ref.shape[1] // 8
    for k in range(tmp.shape[0]):
        for i in range(rows):
            tmp[k, pl.ds(i, 8, stride=rows), :] = values[i * 8 : (i + 1) * 8, 128 * k : 128 * (k + 1)]
        ref[b, :, 128 * k : 128 * (k + 1)] = tmp[k]


def inverse_rms(values):
    return lax.rsqrt(jnp.mean(values * values, -1, keepdims=True) + epsilon)


def norm_back(grad, values):
    scale = inverse_rms(values)
    hat = values * scale
    return scale * (grad - hat * jnp.mean(grad * hat, -1, keepdims=True))


def row_sum(values):
    return jnp.sum(values.reshape(-1, 8, values.shape[-1]), 0)


def extend(ref, edge):
    count = edge.shape[0]
    size = ref.shape[0] - 8 * count
    first = lax.broadcasted_iota(jnp.int32, (8, ref.shape[1]), 0) == 0
    for k in range(count):
        rolled = pltpu.roll(ref[size + 8 * k : size + 8 * (k + 1), :], 1, 0)
        ref[8 * k : 8 * (k + 1), :] = jnp.where(first, edge[k : k + 1], rolled)


def convolve(ext_ref, m_ref, b, taps_ref, r, count):
    taps = taps_ref.shape[0]
    mixed = taps_ref[0:1] * ext_ref[r + 8 * (taps - 1) : r + 8 * (taps - 1) + count, :]
    for j in range(1, taps):
        at = r + 8 * (taps - 1 - j)
        mixed = mixed + taps_ref[j : j + 1] * (m_ref[b, r : r + count, j : j + 1] * ext_ref[at : at + count, :])
    return mixed


def chunk_scan(total, local, back):
    row = lax.broadcasted_iota(jnp.int32, local.shape, 0)
    for dist in (1, 2, 4):
        shift = 8 - dist if back else dist
        valid = (row < 8 - dist) if back else (row >= dist)
        moved_l = pltpu.roll(local, shift, 0)
        moved_t = pltpu.roll(total, shift, 0)
        local = jnp.where(valid, total * moved_l + local, local)
        total = jnp.where(valid, total * moved_t, total)
    shift = 7 if back else 1
    valid = (row < 7) if back else (row >= 1)
    return (
        jnp.where(valid, pltpu.roll(local, shift, 0), 0.0),
        jnp.where(valid, pltpu.roll(total, shift, 0), 1.0),
        local,
        total,
    )


def steps_of(body, n, count):
    if count == 1:
        body(True, True)
        return
    pl.when(n == 0)(lambda: body(True, False))
    if count > 2:
        pl.when((n > 0) & (n < count - 1))(lambda: body(False, False))
    pl.when(n == count - 1)(lambda: body(False, True))


def gates_kernel(natural, layer, *refs):
    x_ref, edge_ref, m_ref, gain_ref, taps_ref, wl_ref, wc_ref, bias_ref = refs[:8]
    sg_ref, sp_ref, eq_ref, own_ref, mth_ref, mtl_ref = refs[8:14]
    rest = list(refs[14:])
    xp_ref = rest.pop(0) if natural else None
    cat_ref, right_ref, ext_ref = rest[:3]
    tmp = rest[3] if natural else None
    batch, size, width = x_ref.shape
    step = sg_ref.shape[-1]
    head = 8 * (taps_ref.shape[0] - 1)
    gain = gain_ref[layer : layer + 1]

    @pl.when(pl.program_id(0) == 0)
    def _():
        def prepare(b, _):
            def put(r, x):
                if natural:
                    xp_ref[b, r : r + 16, :] = x
                ext_ref[head + r : head + r + 16, :] = x * inverse_rms(x) * gain

            load_rows(x_ref, b, tmp, put)
            edge = edge_ref[b]
            extend(ext_ref, edge * inverse_rms(edge) * gain)
            for r in range(0, size, 16):
                mixed = convolve(ext_ref, m_ref, b, taps_ref, r, 16)
                put_left(cat_ref, mixed, pl.ds(pl.multiple_of(b * size + r, 16), 16))
            return _

        lax.fori_loop(0, batch, prepare, 0)

    for k, w_ref in enumerate((wl_ref, wc_ref)):
        high, low = split(w_ref[0])
        for q, part in enumerate((high, high, low)):
            right_ref[q * width : (q + 1) * width, k * step : (k + 1) * step] = part
    bias = bias_ref[layer : layer + 1]

    def product(b):
        return dot(cat_ref[b * size : (b + 1) * size, :], right_ref[...])

    ahead = product(0)
    for b in range(batch):
        now = ahead
        if b + 1 < batch:
            ahead = product(b + 1)
        local = jnp.zeros((8, step), F32)
        total = jnp.ones((8, step), F32)
        for r in range(0, size, 8):
            rows = slice(r, r + 8)
            cand = now[rows, step:]
            gate = 1.0 / (1.0 + jnp.exp(-(now[rows, :step] + bias)))
            soft = jnp.maximum(cand, 0.0) + jnp.log1p(jnp.exp(-jnp.abs(cand)))
            sg_ref[b, rows, :] = gate
            sp_ref[b, rows, :] = soft
            decay = (1.0 - gate) * m_ref[b, rows, 1:2]
            local = decay * local + gate * soft
            total = decay * total
        turn_slice(cat_ref, b, size, pl.program_id(0), mth_ref, mtl_ref)
        parts = chunk_scan(total, local, False)
        eq_ref[b, 0:8, :] = parts[0]
        eq_ref[b, 8:16, :] = parts[1]
        own_ref[0, b : b + 1, :] = parts[3][7:8]
        own_ref[1, b : b + 1, :] = parts[2][7:8]


def gelu_parts(pre):
    sq = pre * pre
    tan = jnp.tanh(pre * (C0 + C1 * sq))
    return sq, tan, 0.5 + 0.5 * tan


def ffn_kernel(natural, layer, first_steps, *refs):
    x_ref, m_ref, sg_ref, sp_ref, eq_ref, inc_ref, wo_ref, gain_ref, up_ref, dn_ref = refs[:10]
    y_ref, last_ref, mid_ref, sth_ref, stl_ref, pre_ref, nth_ref, ntl_ref = refs[10:18]
    cat_ref, ro_ref, ru_ref, rd_ref, act_ref = refs[18:23]
    tmp = refs[23] if natural else None
    batch, size, width = x_ref.shape
    n = pl.program_id(0)

    @pl.when(n < first_steps)
    def _():
        high, low = split(wo_ref[0])
        put_right(ro_ref, high, low, 0)
        group = math.gcd(batch, 3)
        for g in range(0, batch, group):
            block = range(g, g + group)
            state = [eq_ref[b, 0:8] + eq_ref[b, 8:16] * inc_ref[b : b + 1] for b in block]
            for r in range(0, size, 16):
                for k, b in enumerate(block):
                    pair = []
                    for rows in (slice(r, r + 8), slice(r + 8, r + 16)):
                        gate = sg_ref[b, rows, :]
                        decay = (1.0 - gate) * m_ref[b, rows, 1:2]
                        state[k] = decay * state[k] + gate * sp_ref[b, rows, :]
                        pair.append(state[k])
                    rows = slice(b * size + r, b * size + r + 16)
                    sth_ref[rows, :], stl_ref[rows, :] = split(jnp.concatenate(pair, 0))
            for b in block:
                rows = slice(b * size, (b + 1) * size)
                left = jnp.concatenate([sth_ref[rows, :], stl_ref[rows, :], sth_ref[rows, :]], 1)
                mid_ref[b] = dot(left, ro_ref[...]) + jnp.where(n == 0, x_ref[b], mid_ref[b])

    @pl.when(n == first_steps)
    def _():
        gain = gain_ref[layer : layer + 1]

        def prepare(b, _):
            for r in range(0, size, 16):
                middle = mid_ref[b, r : r + 16, :]
                y_ref[b, r : r + 16, :] = middle
                rows = pl.ds(pl.multiple_of(b * size + r, 16), 16)
                put_left(cat_ref, middle * inverse_rms(middle) * gain, rows)
            return _

        lax.fori_loop(0, batch, prepare, 0)

    @pl.when(n >= first_steps)
    def _():
        high, low = split(up_ref[0])
        put_right(ru_ref, high, low, 0)
        high, low = split(dn_ref[0])
        put_right(rd_ref, high, low, 0)

        def product(b):
            return dot(cat_ref[b * size : (b + 1) * size, :], ru_ref[...])

        ahead = product(0)
        for b in range(batch):
            now = ahead
            if b + 1 < batch:
                ahead = product(b + 1)
            act = act_ref.at[b % 2]
            for r in range(0, size, 16):
                pre = now[r : r + 16]
                pre_ref[b * size + r : b * size + r + 16, :] = pre
                put_left(act, pre * gelu_parts(pre)[2], slice(r, r + 16))
            turn_slice(cat_ref, b, size, n - first_steps, nth_ref, ntl_ref)
            y_ref[b] += dot(act[...], rd_ref[...])

    @pl.when(n == pl.num_programs(0) - 1)
    def _():
        count = last_ref.shape[1]

        def finish(b, _):
            for k in range(count):
                row = size - 8 * (count - k) + 7
                last_ref[b, k : k + 1, :] = y_ref[b, row : row + 1, :]
            if natural:
                store_rows(y_ref, b, y_ref[b], tmp)
            return _

        lax.fori_loop(0, batch, finish, 0)


def emit(mine, tile, keep_ref, send_ref, plan, half=0):
    kind, depth, lanes, halves = plan
    if kind == "whole":
        keep_ref[half] = tile
        return
    extra = (0,) if halves == 1 else (half, 0)

    def store(core, ref):
        if kind == "plain":
            zs, ks = ref.shape[-4], ref.shape[-3]
            for z in range(zs):
                for k in range(ks):
                    top = (z * 2 + core) * depth
                    ref[extra + (z, k)] = tile[top : top + depth, 128 * k : 128 * (k + 1)]
        else:
            for r in range(ref.shape[0]):
                for z in range(ref.shape[1]):
                    for k in range(ref.shape[2]):
                        left = (z * 2 + core) * lanes + 128 * k
                        ref[r, z, k] = tile[r * depth : (r + 1) * depth, left : left + 128]

    def stores(core):
        store(core, keep_ref)
        store(1 - core, send_ref)

    pl.when(mine == 0)(lambda: stores(0))
    pl.when(mine != 0)(lambda: stores(1))


def three(high_ref, low_ref):
    return jnp.concatenate([high_ref[...], high_ref[...], low_ref[...]], 0)


def ffn_back_kernel(natural, layer, plans, *refs):
    mine_ref, gy_ref, got_ref, last_ref, first_ref, mid_hbm, gain_ref, nth_hbm, ntl_hbm, pre_ref, dn_ref, up_ref = refs[:12]
    gm_ref, sec_ref, dk_ref, ds_ref, uk_ref, us_ref = refs[12:18]
    cat_ref, gyt_ref, ah_ref, al_ref, gh_ref, gl_ref, rd_ref, ru_ref, gn_ref = refs[18:27]
    mid_ref, nth_ref, ntl_ref, sems = refs[27:31]
    tmp = refs[31] if natural else None
    batch, size, width = gy_ref.shape
    n = pl.program_id(0)
    mine = mine_ref[0]
    gain = gain_ref[layer : layer + 1]
    pairs = ((nth_hbm, nth_ref), (ntl_hbm, ntl_ref), (mid_hbm, mid_ref))
    copies = [pltpu.make_async_copy(a, b, sems.at[k]) for k, (a, b) in enumerate(pairs)]

    @pl.when(n == 0)
    def _():
        for copy in copies:
            copy.start()

        def prepare(b, _):
            start = pl.multiple_of(b * size, size)

            def put(r, gy):
                gm_ref[b, r : r + 16, :] = gy

            load_rows(gy_ref, b, tmp, put)
            if not natural:
                count = last_ref.shape[1]
                at = lax.broadcasted_iota(jnp.int32, (8, width), 0) == 7
                delta = norm_back(got_ref[b] * first_ref[layer + 1 : layer + 2], last_ref[b])
                for k in range(count):
                    row = size - 8 * (count - k)
                    gm_ref[b, row : row + 8, :] += jnp.where(at, delta[k : k + 1], 0.0)
            for r in range(0, size, 16):
                put_left(cat_ref, gm_ref[b, r : r + 16, :], pl.ds(pl.multiple_of(start + r, 16), 16))
            put_left_turned(gyt_ref, gm_ref[b], start)
            return _

        lax.fori_loop(0, batch, prepare, 0)
        sec_ref[...] = jnp.zeros_like(sec_ref)
        gn_ref[...] = jnp.zeros_like(gn_ref)

    high, low = split(dn_ref[0])
    put_right(rd_ref, high, low, 1)
    high, low = split(up_ref[0])
    put_right(ru_ref, high, low, 1)

    def product(b):
        return dot(cat_ref[b * size : (b + 1) * size, :], rd_ref[...], NT)

    ahead = product(0)
    for b in range(batch):
        now = ahead
        if b + 1 < batch:
            ahead = product(b + 1)
        for r in range(0, size, 16):
            rows = slice(b * size + r, b * size + r + 16)
            pre = pre_ref[rows, :]
            sq, tan, half = gelu_parts(pre)
            ah_ref[rows, :], al_ref[rows, :] = split(pre * half)
            slope = half + (0.5 * pre) * (1.0 - tan * tan) * (C0 + (3.0 * C1) * sq)
            gh_ref[rows, :], gl_ref[rows, :] = split(now[r : r + 16] * slope)
        rows = slice(b * size, (b + 1) * size)
        left = jnp.concatenate([gh_ref[rows, :], gl_ref[rows, :], gh_ref[rows, :]], 1)
        gn_ref[rows, :] += dot(left, ru_ref[...], NT)
    emit(mine, dot(gyt_ref[...], three(ah_ref, al_ref)), dk_ref, ds_ref, plans[0])

    @pl.when(n == 0)
    def _():
        copies[0].wait()
        copies[1].wait()

    emit(mine, dot(three_left(nth_ref, ntl_ref), three(gh_ref, gl_ref)), uk_ref, us_ref, plans[1])

    @pl.when(n == pl.num_programs(0) - 1)
    def _():
        copies[2].wait()

        def finish(b, _):
            total = sec_ref[...]
            for r in range(0, size, 16):
                gn = gn_ref[pl.ds(pl.multiple_of(b * size + r, 16), 16), :]
                middle = mid_ref[b, r : r + 16, :]
                scale = inverse_rms(middle)
                hat = middle * scale
                total = total + row_sum(gn * hat)
                gg = gn * gain
                mean = jnp.mean(gg * hat, -1, keepdims=True)
                gm_ref[b, r : r + 16, :] = gm_ref[b, r : r + 16, :] + scale * (gg - hat * mean)
            sec_ref[...] = total
            return _

        lax.fori_loop(0, batch, finish, 0)


def out_back_kernel(afters, *refs):
    gm_ref, m_ref, sg_ref, wo_ref, gs_ref, beq_ref, own_ref, gth_ref, gtl_ref, cat_ref, ro_ref = refs[afters:]
    batch, size, width = gm_ref.shape
    step = sg_ref.shape[-1]
    n = pl.program_id(0)

    def prepare(b):
        for r in range(0, size, 16):
            put_left(cat_ref, gm_ref[b, r : r + 16, :], slice(b * size + r, b * size + r + 16))

    def product(b):
        return dot(cat_ref[b * size : (b + 1) * size, :], ro_ref[...], NT)

    def body(first, _):
        if first:
            prepare(0)
        high, low = split(wo_ref[0])
        put_right(ro_ref, high, low, 1)
        ahead = product(0)
        for b in range(batch):
            gs_ref[b] = ahead
            if b + 1 < batch:
                if first:
                    prepare(b + 1)
                ahead = product(b + 1)
            local = jnp.zeros((8, step), F32)
            total = jnp.ones((8, step), F32)
            for i in reversed(range(size // 8)):
                rows = slice(i * 8, (i + 1) * 8)
                decay = (1.0 - sg_ref[b, rows, :]) * m_ref[b, rows, 1:2]
                local = decay * (gs_ref[b, rows, :] + local)
                total = decay * total
            turn_slice(cat_ref, b, size, n, gth_ref, gtl_ref)
            parts = chunk_scan(total, local, True)
            beq_ref[b, 0:8, :] = parts[0]
            beq_ref[b, 8:16, :] = parts[1]
            own_ref[0, b : b + 1, :] = parts[3][0:1]
            own_ref[1, b : b + 1, :] = parts[2][0:1]

    pl.when(n == 0)(lambda: body(True, False))
    pl.when(n != 0)(lambda: body(False, False))


def out_grad_kernel(plan, mine_ref, gth_ref, gtl_ref, sth_ref, stl_ref, ok_ref, os_ref):
    emit(mine_ref[0], dot(three_left(gth_ref, gtl_ref), three(sth_ref, stl_ref)), ok_ref, os_ref, plan)


def gates_back_kernel(plan, afters, *refs):
    refs = refs[afters:]
    mine_ref, gs_ref, sg_ref, sp_ref, sth_ref, stl_ref, m_ref, beq_ref, ret_ref, inc_ref = refs[:10]
    mth_ref, mtl_ref = refs[10:12]
    glh_ref, gll_ref, gch_ref, gcl_ref, bias_ref, ik_ref, is_ref = refs[12:19]
    batch, size, step = sg_ref.shape
    mine = mine_ref[0]
    top = lax.broadcasted_iota(jnp.int32, (8, step), 0) == 0
    bias_sum = jnp.zeros((8, step), F32)
    group = math.gcd(batch, 2)

    def states(b, r):
        rows = slice(b * size + r, b * size + r + 16)
        return sth_ref[rows, :].astype(F32) + stl_ref[rows, :].astype(F32)

    for g in range(0, batch, group):
        block = range(g, g + group)
        carry = [beq_ref[b, 0:8] + beq_ref[b, 8:16] * ret_ref[b : b + 1] for b in block]
        here = [states(b, size - 16) for b in block]
        wrap = [jnp.where(top, inc_ref[b : b + 1], pltpu.roll(here[k][8:], 1, 0)) for k, b in enumerate(block)]
        for r in reversed(range(0, size, 16)):
            for k, b in enumerate(block):
                below = states(b, r - 16) if r else None
                logits, cands = [], []
                for q in (8, 0):
                    rows = slice(r + q, r + q + 8)
                    prev = here[k][:8] if q else (below[8:] if r else wrap[k])
                    gate = sg_ref[b, rows, :]
                    soft = sp_ref[b, rows, :]
                    other = 1.0 - gate
                    adjoint = gs_ref[b, rows, :] + carry[k]
                    through = adjoint * m_ref[b, rows, 1:2]
                    carry[k] = other * through
                    glogit = gate * other * (adjoint * soft - through * prev)
                    bias_sum = bias_sum + glogit
                    logits.insert(0, glogit)
                    cands.insert(0, adjoint * gate * (1.0 - jnp.exp(-soft)))
                here[k] = below
                rows = slice(b * size + r, b * size + r + 16)
                glh_ref[rows, :], gll_ref[rows, :] = split(jnp.concatenate(logits, 0))
                gch_ref[rows, :], gcl_ref[rows, :] = split(jnp.concatenate(cands, 0))
    bias_ref[...] = bias_sum
    right = jnp.concatenate([three(glh_ref, gll_ref), three(gch_ref, gcl_ref)], 1)
    tile = dot(three_left(mth_ref, mtl_ref), right)
    for half in range(2):
        emit(mine, tile[:, half * step : (half + 1) * step], ik_ref, is_ref, plan, half)


def conv_back_kernel(natural, layer, batch, afters, *refs):
    refs = refs[afters:]
    glh_ref, gll_ref, gch_ref, gcl_ref, m_ref, x_ref, edge_ref, gm_ref, taps_ref, gain_ref, w_ref = refs[:11]
    gx_ref, send_ref, s_ref = refs[11:14]
    right_ref, acc_ref, ext_ref, out_ref = refs[14:18]
    tmp = refs[18] if natural else None
    _, size, width = x_ref.shape
    taps = taps_ref.shape[0]
    head = 8 * (taps - 1)
    n = pl.program_id(0)

    def product(slot):
        high = jnp.concatenate([glh_ref[...], gch_ref[...]], 1)
        low = jnp.concatenate([gll_ref[...], gcl_ref[...]], 1)
        acc_ref[slot] = dot(jnp.concatenate([high, low, high], 1), right_ref[...], NT)

    def finish(slot):
        b = n - 1
        last = lax.broadcasted_iota(jnp.int32, (8, width), 0) == 7
        gain = gain_ref[layer : layer + 1]
        scales = []
        for r in range(0, size, 8):
            x = x_ref[0, r : r + 8, :]
            scales.append(inverse_rms(x))
            ext_ref[head + r : head + r + 8, :] = x * scales[-1]
        edge = edge_ref[b]
        extend(ext_ref, edge * inverse_rms(edge))

        def scaled(j, r):
            return taps_ref[j : j + 1] * (m_ref[b, r : r + 8, j : j + 1] * acc_ref[slot, r : r + 8, :])

        sends = [None] * taps
        tails = {}
        for j in range(1, taps):
            for k in range(j):
                piece = scaled(j, 8 * k)
                tails[j, k] = jnp.where(last, 0.0, pltpu.roll(piece, 7, 0))
                sends[j - k] = piece if sends[j - k] is None else sends[j - k] + piece
        for k in range(1, taps):
            send_ref[b, taps - 1 - k : taps - k, :] = sends[k][0:1]
        sums = [s_ref[8 * j : 8 * (j + 1)] for j in range(taps)]
        for r in range(0, size, 8):
            gmixed = acc_ref[slot, r : r + 8, :]
            hat = ext_ref[head + r : head + r + 8, :]
            gn = taps_ref[0:1] * gmixed
            sums[0] = sums[0] + gmixed * hat
            for j in range(1, taps):
                at = head + r - 8 * j
                sums[j] = sums[j] + m_ref[b, r : r + 8, j : j + 1] * gmixed * ext_ref[at : at + 8, :]
                ahead = r + 8 * j
                gn = gn + (scaled(j, ahead) if ahead < size else tails[j, (ahead - size) // 8])
            gg = gn * gain
            mean = jnp.mean(gg * hat, -1, keepdims=True)
            gx = gm_ref[0, r : r + 8, :] + scales[r // 8] * (gg - hat * mean)
            if natural:
                out_ref[r : r + 8, :] = gx
            else:
                gx_ref[0, r : r + 8, :] = gx
        for j in range(taps):
            s_ref[8 * j : 8 * (j + 1)] = sums[j]
        if natural:
            store_rows(gx_ref, 0, out_ref[...], tmp)

    @pl.when(n == 0)
    def _():
        s_ref[...] = jnp.zeros_like(s_ref)
        high, low = split(w_ref[0])
        put_right(right_ref, high, low, 1)
        product(0)

    for odd in range(2):

        @pl.when((n > 0) & (n < batch) & (n % 2 == odd))
        def _():
            product(odd)
            finish(1 - odd)

    @pl.when(n == batch)
    def _():
        finish((batch - 1) % 2)


def add_kernel(count, afters, *refs):
    refs = refs[afters:]
    out_ref = refs[2 * count]
    start = 0
    for k in range(count):
        rows = refs[2 * k].shape[-2]
        out_ref[:, :, start : start + rows, :] = refs[2 * k][...] + refs[2 * k + 1][...]
        start += rows


def shape(*dims, dtype=F32):
    return jax.ShapeDtypeStruct(dims, dtype)


def fixed(array):
    zero = (0,) * len(array.shape)
    return (array, pl.BlockSpec(array.shape, lambda n: zero, pipeline_mode=pl.Buffered(1)))


def in_hbm(array):
    return (array, pl.BlockSpec(memory_space=pltpu.HBM))


def out_fixed(*dims):
    zero = (0,) * len(dims)
    return (shape(*dims), pl.BlockSpec(dims, lambda n: zero))


def chunked(array, at=lambda n: n, axis=-1, layer=None, step=CHUNK):
    dims = list(array.shape)
    axis = axis % len(dims)
    dims[axis] = step
    if layer is not None:
        dims[0] = 1

    def index(n):
        place = [0] * len(dims)
        place[axis] = at(n)
        if layer is not None:
            place[0] = layer
        return tuple(place)

    return (array, pl.BlockSpec(tuple(dims), index))


def block_bytes(dims, dtype):
    dims = [1 if d is None else d for d in dims]
    size = jnp.dtype(dtype).itemsize
    dims[-1] = -(-dims[-1] // 128) * 128
    if len(dims) > 1:
        dims[-2] = -(-dims[-2] // 8) * 8
    return math.prod(dims) * size


def vmem_need(ins, outs, scratch):
    total = 8 * 1024 * 1024
    for array, spec in list(ins) + list(outs):
        if spec.block_shape is not None:
            total += block_bytes(spec.block_shape, array.dtype) * (2 if spec.pipeline_mode is None else 1)
    for ref in scratch:
        if ref.memory_space == pltpu.VMEM:
            total += block_bytes(ref.shape, ref.dtype)
    return min(total, VMEM)


def call(kernel, grid, ins, outs, scratch=(), flops=0, name=None, free=False):
    def large(array):
        return math.prod(array.shape) * array.dtype.itemsize > LARGE

    args = [
        pltpu.with_memory_space_constraint(array, pltpu.HBM)
        if spec.memory_space == pltpu.HBM or (spec.memory_space is None and large(array) and not free)
        else array
        for array, spec in ins
    ]
    shapes = [pltpu.HBM(array.shape, array.dtype) if large(array) and not free else array for array, _ in outs]
    moved = sum(math.prod(a.shape) * a.dtype.itemsize for a, _ in ins)
    moved += sum(math.prod(a.shape) * a.dtype.itemsize for a, _ in outs)
    return pl.pallas_call(
        kernel,
        grid=(grid,),
        in_specs=[s for _, s in ins],
        out_specs=[s for _, s in outs],
        out_shape=shapes,
        scratch_shapes=list(scratch),
        compiler_params=pltpu.CompilerParams(
            vmem_limit_bytes=vmem_need(ins, outs, scratch), dimension_semantics=("arbitrary",)
        ),
        cost_estimate=pl.CostEstimate(flops=int(flops), bytes_accessed=int(moved), transcendentals=0),
        name=name,
    )(*args)


def kept_back(arrays):
    return [in_hbm(a) for a in arrays]


def shift(block, distance):
    size = lax.axis_size("seq")
    route = [(i - distance, i) for i in range(size) if 0 <= i - distance < size]
    return lax.ppermute(block, "seq", route)


def partner(block, flip):
    return lax.ppermute(block, "seq", [(i, i ^ flip) for i in range(lax.axis_size("seq"))])


def combine(earlier, later):
    return jnp.stack([earlier[0] * later[0], later[0] * earlier[1] + later[1]])


def carry_kernel(afters, flag_ref, first_ref, second_ref, out_ref):
    swap = flag_ref[0] == 0
    first, second = first_ref[...], second_ref[...]
    earlier = jnp.where(swap, second, first)
    later = jnp.where(swap, first, second)
    out_ref[0] = earlier[0] * later[0]
    out_ref[1] = later[0] * earlier[1] + later[1]


def joined_carry(first, second, flag, afters):
    def kernel(*refs):
        carry_kernel(0, *refs[len(afters) :])

    flag = (flag.astype(jnp.int32).reshape(1), pl.BlockSpec(memory_space=pltpu.SMEM))
    return call(
        kernel,
        1,
        kept_back(afters) + [flag, fixed(first), fixed(second)],
        [out_fixed(*first.shape)],
        name="carry",
    )[0]


def incoming_carry(own, back, fillers=((), ())):
    size = lax.axis_size("seq")
    other = partner(own, 1)
    odd = lax.axis_index("seq") % 2 == 1
    is_later = ~odd if back else odd
    if back:
        pair = joined_carry(other, own, is_later, fillers[0])
    else:
        pair = jnp.where(is_later, combine(other, own), combine(own, other))
    sign = -2 if back else 2
    before = None
    dist = 1
    while dist < size // 2:
        got = shift(pair, sign * dist)
        before = got if before is None else combine(got, before)
        if 2 * dist < size // 2:
            if back and dist == 1:
                pair = joined_carry(got, pair, jnp.ones((), jnp.int32), fillers[1])
            else:
                pair = combine(got, pair)
        dist *= 2
    enters = jnp.where(is_later, other[0] * before[1] + other[1], before[1])
    return (enters, pair) if back else enters


def document_masks(starts_rows, group):
    place = jnp.arange(group, dtype=jnp.int32)
    position = lax.axis_index("seq") * group + (place % 8) * (group // 8) + place // 8
    back = position[:, None] - jnp.arange(8, dtype=jnp.int32)

    def document(at):
        return sum((starts_rows[:, k, None, None] <= at).astype(jnp.int32) for k in range(starts_rows.shape[1]))

    return (document(back) == document(position[:, None])).astype(F32)


class Grad:
    def __init__(self, height, width, flip, direct, step, halves=1):
        self.rows = lax.axis_size("rows")
        self.seq = lax.axis_size("seq")
        self.flip = flip
        self.direct = direct
        self.height = height
        self.width = width
        self.depth = height // (self.rows if flip else self.seq)
        self.lanes = width * halves // (self.seq if flip else self.rows)
        zs = self.seq // 2
        if not direct:
            self.plan = ("whole", 0, 0, halves)
            self.out = (shape(halves, height, width), pl.BlockSpec((halves, height, step), lambda n: (0, 0, n)))
        elif flip:
            self.plan = ("flip", self.depth, self.lanes, 1)
            ks = self.lanes // 128
            dims = (self.rows, zs, ks, self.depth, 128)
            block = (self.rows, step // (2 * self.lanes), ks, self.depth, 128)
            self.out = (shape(*dims), pl.BlockSpec(block, lambda n: (0, n, 0, 0, 0)))
        else:
            self.plan = ("plain", self.depth, self.lanes, halves)
            per = self.lanes // step
            dims = (self.rows // halves, zs, self.lanes // 128, self.depth, 128)
            block = (1, zs, step // 128, self.depth, 128)
            if halves == 1:
                self.out = (shape(*dims), pl.BlockSpec(block, lambda n: (n // per, 0, n % per, 0, 0)))
            else:
                spec = pl.BlockSpec((halves,) + block, lambda n: (0, n // per, 0, n % per, 0, 0))
                self.out = (shape(halves, *dims), spec)

    def outs(self):
        return [self.out, self.out if self.direct else out_fixed(8, 128)]

    def pieces(self, array):
        return array.reshape(self.rows, self.seq // 2, -1, 128)

    def whole(self, array):
        out = array.reshape(self.lanes // 128, self.depth, 128).swapaxes(0, 1).reshape(self.depth, self.lanes)
        return out.T if self.flip else out

    def plain_sum(self, value):
        value = jnp.concatenate(list(value), 1)
        value = lax.psum_scatter(value, "seq", scatter_dimension=1 if self.flip else 0, tiled=True)
        value = lax.psum_scatter(value, "rows", scatter_dimension=0 if self.flip else 1, tiled=True)
        return value.T if self.flip else value


def butterfly(value):
    for axis in ("seq", "rows"):
        size = lax.axis_size(axis)
        flip = 1
        while flip < size:
            value = value + lax.ppermute(value, axis, [(i, i ^ flip) for i in range(size)])
            flip *= 2
    return value


def pair_sum(parts, afters=()):
    ins = []
    for kept, sent in parts:
        got = partner(sent, 1)
        ins += [kept, got]
    count = len(parts)
    rows, zs = ins[0].shape[:2]
    total = sum(a.shape[2] for a in ins[::2])
    return call(
        functools.partial(add_kernel, count, len(afters)),
        rows,
        kept_back(afters)
        + [(a, pl.BlockSpec((1,) + a.shape[1:], lambda n: (n, 0, 0, 0))) for a in ins],
        [(shape(rows, zs, total, 128), pl.BlockSpec((1, zs, total, 128), lambda n: (n, 0, 0, 0)))],
        name="neighbour_sum",
        free=True,
    )[0]


def reduce_rows(pieces):
    return lax.psum_scatter(pieces, "rows", scatter_dimension=0, tiled=True)[0]


def seq_step(arrays, dist, got=None, afters=()):
    count = len(arrays)
    places = arrays[0].shape[0]
    total = sum(a.shape[1] for a in arrays)
    bit = ((lax.axis_index("seq") // 2 // dist) % 2).astype(jnp.int32).reshape(1)

    def kernel(*refs):
        refs = refs[len(afters) :]
        own = refs[0][0]
        ins = refs[1 : 1 + count]
        more = refs[1 + count] if got is not None else None
        outs = refs[1 + count + (got is not None) :]
        start = 0
        for ref in ins:
            rows = ref.shape[1]
            for z in range(places):
                value = ref[z]
                if more is not None:
                    value = value + more[z, start : start + rows, :]
                if places == 1:
                    outs[0][0, start : start + rows, :] = value
                    continue

                def put(ref, value=value, start=start, rows=rows, z=z):
                    ref[z // 2, start : start + rows, :] = value

                pl.when(own == z % 2)(functools.partial(put, outs[0]))
                pl.when(own != z % 2)(functools.partial(put, outs[1]))
            start += rows

    half = max(1, places // 2)
    return call(
        kernel,
        1,
        kept_back(afters)
        + [(bit, pl.BlockSpec(memory_space=pltpu.SMEM))]
        + [fixed(a) for a in arrays]
        + ([fixed(got)] if got is not None else []),
        [out_fixed(half, total, 128) for _ in range(2 if places > 1 else 1)],
        name="seq_sum",
        free=True,
    )


def reduce_seq(kept, afters=()):
    dist = 1
    while len(kept) == 2:
        got = partner(kept[1], 2 * dist)
        dist *= 2
        kept = seq_step([kept[0]], dist, got, afters)
    return kept[0][0]


def per_device(
    inputs,
    starts,
    first_gain,
    conv_taps,
    in_weight,
    gate_bias,
    out_weight,
    second_gain,
    up_weight,
    down_weight,
    cotangent,
):
    dims = inputs.shape
    batch = dims[0] * dims[1]
    group = dims[2]
    width = dims[3]
    tokens = batch * group
    taps = conv_taps.shape[2]
    layers = in_weight.shape[0]
    hidden = out_weight.shape[1]
    ff = up_weight.shape[2]
    rows_size, seq_size = lax.axis_size("rows"), lax.axis_size("seq")
    direct = (
        ff % (CHUNK * rows_size) == 0
        and (2 * hidden) % (HALF * rows_size) == 0
        and rows_size % 2 == 0
        and all(n % (128 * seq_size) == 0 and CHUNK % (2 * n // seq_size) == 0 for n in (ff, hidden))
    )
    extended = pltpu.VMEM((8 * (taps - 1) + group, width), F32)
    order = [pltpu.VMEM((width // 128, group, 128), F32)]
    mine = (lax.axis_index("seq") % 2).astype(jnp.int32).reshape(1)
    mine = (mine, pl.BlockSpec(memory_space=pltpu.SMEM))
    masks = document_masks(starts.reshape(batch, -1), group)
    taps_rows = conv_taps.swapaxes(1, 2)
    in_flops = 6 * tokens * width * 2 * hidden
    out_flops = 6 * tokens * width * hidden
    ffn_flops = 6 * tokens * width * ff * 2

    current = inputs.reshape(batch, group, width)
    last_rows = current[:, group - taps + 1 :]
    row_hidden = shape(batch, group, hidden)
    row_eq = shape(batch, 16, hidden)
    row_own = shape(2, batch, hidden)
    turned = shape(width, tokens, dtype=BF)
    saved = []
    for layer in range(layers):
        natural = layer == 0
        final = layer == layers - 1
        edge = shift(last_rows, 1)
        steps = hidden // CHUNK
        res = call(
            functools.partial(gates_kernel, natural, layer),
            steps,
            [fixed(current), fixed(edge), fixed(masks), fixed(first_gain), fixed(taps_rows[layer])]
            + [chunked(in_weight, layer=layer), chunked(in_weight, lambda n: n + steps, layer=layer)]
            + [chunked(gate_bias)],
            [chunked(row_hidden), chunked(row_hidden), chunked(row_eq), chunked(row_own)]
            + [chunked(turned, axis=0, step=width // steps) for _ in range(2)]
            + ([out_fixed(batch, group, width)] if natural else []),
            scratch=[pltpu.VMEM((tokens, 3 * width), BF), pltpu.VMEM((3 * width, 2 * CHUNK), BF), extended]
            + (order if natural else []),
            flops=in_flops,
            name="gates",
        )
        sg, sp, eq, own = res[:4]
        mixt = res[4:6]
        x = res[6] if natural else current
        inc = incoming_carry(own, False)
        early_steps = hidden // HALF

        def early(n):
            return jnp.minimum(n, early_steps - 1)

        def late(n):
            return jnp.maximum(n - early_steps, 0)

        def halves(array):
            return chunked(array, early, step=HALF)

        res = call(
            functools.partial(ffn_kernel, final, layer, early_steps),
            early_steps + ff // CHUNK,
            [fixed(x), fixed(masks), halves(sg), halves(sp), halves(eq), halves(inc)]
            + [chunked(out_weight, early, axis=1, layer=layer, step=HALF), fixed(second_gain)]
            + [chunked(up_weight, late, layer=layer), chunked(down_weight, late, axis=1, layer=layer)],
            [
                out_fixed(batch, group, width),
                out_fixed(batch, taps - 1, width),
                out_fixed(batch, group, width),
                halves(shape(tokens, hidden, dtype=BF)),
                halves(shape(tokens, hidden, dtype=BF)),
                chunked(shape(tokens, ff), late),
                chunked(turned, late, axis=0, step=width // (ff // CHUNK)),
                chunked(turned, late, axis=0, step=width // (ff // CHUNK)),
            ],
            scratch=[
                pltpu.VMEM((tokens, 3 * width), BF),
                pltpu.VMEM((3 * HALF, width), BF),
                pltpu.VMEM((3 * width, CHUNK), BF),
                pltpu.VMEM((3 * CHUNK, width), BF),
                pltpu.VMEM((2, group, 3 * CHUNK), BF),
            ]
            + (order if final else []),
            flops=out_flops + ffn_flops,
            name="ffn",
        )
        current, following, mid, st, pre, nt = res[0], res[1], res[2], res[3:5], res[5], res[6:8]
        saved.append((x, last_rows, edge, sg, sp, inc, mid, st, pre, mixt, nt))
        last_rows = following
    outputs = current

    grad = cotangent.reshape(batch, group, width)
    got = jnp.zeros((batch, taps - 1, width), F32)
    down_plan = Grad(width, ff, True, direct, CHUNK)
    up_plan = Grad(width, ff, False, direct, CHUNK)
    out_plan = Grad(width, hidden, True, direct, CHUNK)
    in_plan = Grad(width, hidden, False, direct, HALF, 2)
    shards = [None] * layers
    smalls = [None] * layers
    early_rows = [None] * layers
    late_rows = [None] * layers
    for layer in reversed(range(layers)):
        x, last_rows, edge, sg, sp, inc, mid, st, pre, mixt, nt = saved[layer]
        final = layer == layers - 1
        first = layer == 0
        above = last_rows if final else saved[layer + 1][1]
        res = call(
            functools.partial(ffn_back_kernel, final, layer, (down_plan.plan, up_plan.plan)),
            ff // CHUNK,
            [mine, fixed(grad), fixed(got), fixed(above), fixed(first_gain)]
            + [in_hbm(mid), fixed(second_gain), in_hbm(nt[0]), in_hbm(nt[1]), chunked(pre)]
            + [chunked(down_weight, axis=1, layer=layer), chunked(up_weight, layer=layer)],
            [out_fixed(batch, group, width), out_fixed(8, width)] + down_plan.outs() + up_plan.outs(),
            scratch=[
                pltpu.VMEM((tokens, 3 * width), BF),
                pltpu.VMEM((width, 3 * tokens), BF),
                pltpu.VMEM((tokens, CHUNK), BF),
                pltpu.VMEM((tokens, CHUNK), BF),
                pltpu.VMEM((tokens, CHUNK), BF),
                pltpu.VMEM((tokens, CHUNK), BF),
                pltpu.VMEM((CHUNK, 3 * width), BF),
                pltpu.VMEM((width, 3 * CHUNK), BF),
                pltpu.VMEM((tokens, width), F32),
                pltpu.VMEM((batch, group, width), F32),
                pltpu.VMEM((width, tokens), BF),
                pltpu.VMEM((width, tokens), BF),
                pltpu.SemaphoreType.DMA((3,)),
            ]
            + (order if final else []),
            flops=2 * ffn_flops,
            name="ffn_back",
        )
        gm, sec, down_g, up_g = res[0], res[1], res[2:4], res[4:6]
        waiting = []
        z_next = None
        if direct and not final:
            z_next = seq_step([early_rows[layer + 1], late_rows[layer + 1]], 1, None, [gm])
            waiting = [z_next[1]]
        res = call(
            functools.partial(out_back_kernel, len(waiting)),
            hidden // CHUNK,
            kept_back(waiting) + [fixed(gm), fixed(masks), chunked(sg), chunked(out_weight, axis=1, layer=layer)],
            [chunked(row_hidden), chunked(row_eq), chunked(row_own)]
            + [chunked(turned, axis=0, step=width // (hidden // CHUNK)) for _ in range(2)],
            scratch=[pltpu.VMEM((tokens, 3 * width), BF), pltpu.VMEM((CHUNK, 3 * width), BF)],
            flops=out_flops,
            name="out_back",
        )
        gs, beq, own, gmt = res[0], res[1], res[2], res[3:5]
        out_g = call(
            functools.partial(out_grad_kernel, out_plan.plan),
            hidden // CHUNK,
            [mine, fixed(gmt[0]), fixed(gmt[1]), chunked(st[0]), chunked(st[1])],
            out_plan.outs(),
            flops=out_flops,
            name="out_grad",
        )
        waiting = []
        fillers = [[], list(out_g)]
        if direct:
            early_parts = [tuple(down_plan.pieces(v) for v in down_g), tuple(up_plan.pieces(v) for v in up_g)]
            if first:
                early = pair_sum(early_parts, [gs])
                early_rows[layer] = reduce_rows(early)
                fillers[0].append(early)
        ret, last_pair = incoming_carry(own, True, fillers)
        if direct and not first:
            early = pair_sum(early_parts, [last_pair])
            early_rows[layer] = reduce_rows(early)
            waiting.append(early)
        if z_next is not None:
            z_next = seq_step([z_next[0]], 2, partner(z_next[1], 2), [last_pair])
            waiting.append(z_next[-1])
        steps = hidden // HALF
        halves = functools.partial(chunked, step=HALF)
        res = call(
            functools.partial(gates_back_kernel, in_plan.plan, len(waiting)),
            steps,
            kept_back(waiting)
            + [mine, halves(gs), halves(sg), halves(sp), halves(st[0]), halves(st[1]), fixed(masks)]
            + [halves(beq), halves(ret), halves(inc)]
            + [fixed(mixt[0]), fixed(mixt[1])],
            [halves(shape(tokens, hidden, dtype=BF)) for _ in range(4)] + [halves(shape(8, hidden))] + in_plan.outs(),
            flops=in_flops,
            name="gates_back",
        )
        gproj, bias_sum, in_g = res[:4], res[4], res[5:7]
        waiting = []
        late_parts = None
        if direct:
            late_parts = [tuple(out_plan.pieces(v) for v in out_g), tuple(in_plan.pieces(v) for v in in_g)]
            if first:
                halved = seq_step([early_rows[layer]], 1, None, [bias_sum])
                late = pair_sum(late_parts, [halved[-1]])
                late_rows[layer] = reduce_rows(late)
                waiting = [late]

        def now(n):
            return jnp.minimum(n, batch - 1)

        def lag(n):
            return jnp.maximum(n - 1, 0)

        res = call(
            functools.partial(conv_back_kernel, first, layer, batch, len(waiting)),
            batch + 1,
            kept_back(waiting)
            + [chunked(g, now, axis=0, step=group) for g in gproj]
            + [fixed(masks), chunked(x, lag, axis=0, step=1), fixed(edge), chunked(gm, lag, axis=0, step=1)]
            + [fixed(taps_rows[layer]), fixed(first_gain)]
            + [(in_weight, pl.BlockSpec((1, width, 2 * hidden), lambda n: (layer, 0, 0), pipeline_mode=pl.Buffered(1)))],
            [
                chunked(shape(batch, group, width), lag, axis=0, step=1),
                out_fixed(batch, taps - 1, width),
                out_fixed(8 * taps, width),
            ],
            scratch=[pltpu.VMEM((width, 6 * hidden), BF), pltpu.VMEM((2, group, width), F32)]
            + [extended, pltpu.VMEM((group, width), F32)]
            + (order if first else []),
            flops=in_flops,
            name="conv_back",
        )
        grad, send, sums = res
        if z_next is not None:
            dist = 2
            while len(z_next) == 2:
                got = partner(z_next[1], 2 * dist)
                dist *= 2
                z_next = seq_step([z_next[0]], dist, got, [grad])
            early_rows[layer + 1] = z_next[0][0]
        if direct and not first:
            late_rows[layer] = reduce_rows(pair_sum(late_parts, [grad]))
        if not direct:
            shards[layer] = (
                in_plan.plain_sum(in_g[0]),
                out_plan.plain_sum(out_g[0]),
                up_plan.plain_sum(up_g[0]),
                down_plan.plain_sum(down_g[0]),
            )
        got = shift(send, -1)
        if first:
            grad = grad.at[:, group - taps + 1 :].add(norm_back(got * first_gain[layer], last_rows))
        smalls[layer] = jnp.concatenate(
            [
                jnp.sum(sums.reshape(taps, 8, width), 1),
                jnp.sum(sec, 0, keepdims=True),
                jnp.sum(bias_sum, 0).reshape(-1, width),
            ],
            0,
        )

    if direct:
        down_k = down_plan.depth * down_plan.lanes // 128
        up_k = up_plan.depth * up_plan.lanes // 128
        out_k = out_plan.depth * out_plan.lanes // 128
        done = early_rows[1:]
        early = reduce_seq(halved, [sums])
        late = reduce_seq(seq_step([late_rows[0]], 1))
        done.insert(0, jnp.concatenate([early, late], 0))
        for layer in range(layers):
            parts = jnp.split(done[layer], [down_k, down_k + up_k, down_k + up_k + out_k])
            plans = (down_plan, up_plan, out_plan, in_plan)
            shards[layer] = tuple(plan.whole(part) for plan, part in zip(plans, parts))[::-1]
    in_grad, out_grad, up_grad, down_grad = (jnp.stack([s[k] for s in shards]) for k in range(4))
    every = butterfly(jnp.stack(smalls))
    sums = every[:, :taps]
    first_grad = jnp.sum(sums * taps_rows, 1)
    taps_grad = (sums * first_gain[:, None]).swapaxes(1, 2)
    second_grad = every[:, taps]
    bias_grad = every[:, taps + 1 :].reshape(layers, hidden)
    return (
        outputs.reshape(dims),
        grad.reshape(dims),
        first_grad,
        taps_grad,
        in_grad,
        bias_grad,
        out_grad,
        second_grad,
        up_grad,
        down_grad,
    )


def solution(mesh):
    in_specs = (
        P(None, "rows", "seq", None),
        P(None, "rows", None),
        P(),
        P(),
        P(),
        P(),
        P(),
        P(),
        P(),
        P(),
        P(None, "rows", "seq", None),
    )
    out_specs = (
        P(None, "rows", "seq", None),
        P(None, "rows", "seq", None),
        P(),
        P(),
        P(None, "seq", "rows"),
        P(),
        P(None, "seq", "rows"),
        P(),
        P(None, "seq", "rows"),
        P(None, "seq", "rows"),
    )
    return jax.shard_map(
        per_device, mesh=mesh, in_specs=in_specs, out_specs=out_specs, check_vma=False
    )
```

time: 2870 us -> 555 us (0.19); the launches traced: 2810 us -> 548 us
  local copies, waits for them, and re-layouts: 1560 us -> 27.4 us
  matrix products: 550 us -> 0 us
  other arithmetic: 397 us -> 8.5 us
  Pallas kernels: 0 us -> 380 us
  waiting for transfers between devices: 160 us -> 60.2 us
  blocking collectives: 38.7 us -> 0 us
  starting transfers between devices: 87.1 us -> 57.4 us
    slice x227 -> x2, local copies, waits for them, and re-layouts: 903 us -> 0.01 us  [the longest x1 0.01 us: per_device(): second_grad = every[:, taps]]
    dot_general x24 -> x0, matrix products: 550 us -> none  [the longest x8 199 us: project_back(): jnp.einsum('bck,jk->bcj', left, right, precision=lax.Precision.HIGHEST)]
    pad x112 -> x0, local copies, waits for them, and re-layouts: 402 us -> none  [the longest x56 231 us: layer_forward(): total, local = lax.associative_scan(combine_pairs, (decay, drive), axis=1)]
    pallas_call x0 -> x31, Pallas kernels: none -> 380 us  [call(): pl.pallas_call(kernel, grid=(grid,), in_specs=[s for _, s in ins], out_sp...]
    add x132 -> x9, other arithmetic: 219 us -> 0.14 us  [the longest x1 0.08 us: document(): sum(((starts_rows[:, k, None, None] <= at).astype(jnp.int32) for k in ran...]
    rev x4 -> x0, local copies, waits for them, and re-layouts: 194 us -> none  [layer_backward(): lax.associative_scan(combine_pairs, (following, state_grad), axis=1, reve...]
    reduce_scatter x8 -> x0, waiting for transfers between devices: 89.1 us -> none  [the longest x1 31.5 us: per_device(): lax.psum_scatter(partial_sums[0], 'rows', scatter_dimension=2, tiled=True)]
    mul x36 -> x2, other arithmetic: 73.2 us -> 0.02 us  [combine(): return jnp.stack([earlier[0] * later[0], later[0] * earlier[1] + later[1]])]
  transfers between devices with their start and end apart: 40 -> 39, of which waited for: 34 -> 23; matrix products, arithmetic and copies ran while one was open for 29% -> 2% of each run, Pallas kernels for 0% -> 35%
where the time goes in v1:
time: 555 us; the launch traced here: 548 us
  Pallas kernels  380 us (68%)
  waiting for transfers between devices  60.2 us (11%)
  starting transfers between devices  57.4 us (10%)
  local copies, waits for them, and re-layouts  27.4 us (5%)
  between operations  15.2 us (3%)
  other arithmetic  8.5 us (2%)
    pallas_call x31, Pallas kernels, call(): pl.pallas_call(kernel, grid=(grid,), in_specs=[s for _, s in ins], out_sp...  380 us
    ppermute x12, waiting for transfers between devices, shift(): return lax.ppermute(block, 'seq', route)  31.9 us
    ppermute x12, starting transfers between devices, shift(): return lax.ppermute(block, 'seq', route)  31.2 us
    unnamed x107, local copies, waits for them, and re-layouts  23.5 us
    ppermute x18, waiting for transfers between devices, partner(): lax.ppermute(block, 'seq', [(i, i ^ flip) for i in range(lax.axis_size('s...  22 us
    ppermute x18, starting transfers between devices, partner(): lax.ppermute(block, 'seq', [(i, i ^ flip) for i in range(lax.axis_size('s...  18.5 us
  transfers between devices with their start and end apart: 39, of which 23 were waited for; matrix products, arithmetic and copies ran while one was open for 2% of the time, Pallas kernels for 35%

profile of v1, /device:TPU:0, one launch (start us, length us, event | category | flops | bytes accessed | tf_op | source)
XLA Modules:
  0.0 548.3 jit_solution(13387756906217403436)
XLA Ops:
  8.8 2.3 collective-permute-start
  14.6 24.0 %gates.2 = (f32[6,256,1024]{2,1,0:T(8,128)}, f32[6,256,1024]{2,1,0:T(8,128)}, f32[6,16,1024]{2,1,0:T(8,128)}, f32[2,6,1024]{2,1,0:T(8,128)S(1)}, bf16[512,1536]{...) custom-call(f32[6,256,512]{2,1,0:T(8,128)} %bitcast.195, ...), custom_call_target="tpu_custom_call" | custom-call | flops 9663676416 | bytes 39346176 | tf_op jit(solution)/shard_map/gates/pallas_call | solution.py:695
  38.7 2.7 collective-permute-start.1
  42.3 3.6 collective-permute-start.2
  46.0 1.9 collective-permute-done.2
  47.9 5.6 %collective-permute-start.3 = (f32[2,6,1024]{2,1,0:T(8,128)S(1)}, f32[2,6,1024]{2,1,0:T(8,128)S(1)}, u32[]{:S(2)}, u32[]{:S(2)}) collective-permute-start(f32[2,6,1024]{2,1,0:T(8,128)S(1)} %pad_maximum_fusion.8), channel_id=1, source_target_pairs={{0,4},{1,5},{2,6},{3,7},{8,12},{9,13},{10,14},{11,15},{16,20},{17,... | collective-permute-start | bytes 147464 | tf_op jit(solution)/shard_map/ppermute | solution.py:717
  53.5 1.6 collective-permute-done.3
  55.7 38.9 %ffn.2 = (f32[6,256,512]{2,1,0:T(8,128)}, f32[6,3,512]{2,1,0:T(4,128)}, f32[6,256,512]{2,1,0:T(8,128)}, bf16[1536,1024]{1,0:T(8,128)(2,1)}, bf16[1536,1024]{1,0:...) custom-call(f32[6,256,512]{2,1,0:T(8,128)} %get-tuple-element.108.refs_0_.refs_6_, ...), custom_call_target="tpu_custom_call" | custom-call | flops 24159191040 | bytes 65519616 | tf_op jit(solution)/shard_map/ffn/pallas_call | solution.py:695
  94.6 1.8 collective-permute-start.4
  97.0 21.2 %gates.3 = (f32[6,256,1024]{2,1,0:T(8,128)}, f32[6,256,1024]{2,1,0:T(8,128)}, f32[6,16,1024]{2,1,0:T(8,128)}, f32[2,6,1024]{2,1,0:T(8,128)S(1)}, bf16[512,1536]{1,0:T(8,128)(2,1)}, /*index=5*/bf16[512,1536]{1,0:T(8,128)(2,1)}) custom-call(f32[6,256,512]{2,1,0:T(8,128)} %get-tuple-element.113.refs_0_.refs_5_, ...), custom_call_target="tpu_custom_call" | custom-call | flops 9663676416 | bytes 36200448 | tf_op jit(solution)/shard_map/gates/pallas_call | solution.py:695
  118.2 3.2 collective-permute-start.5
  122.3 4.4 collective-permute-start.6
  126.7 1.9 collective-permute-done.6
  128.6 5.7 %collective-permute-start.7 = (f32[2,6,1024]{2,1,0:T(8,128)S(1)}, f32[2,6,1024]{2,1,0:T(8,128)S(1)}, u32[]{:S(2)}, u32[]{:S(2)}) collective-permute-start(f32[2,6,1024]{2,1,0:T(8,128)S(1)} %pad_maximum_fusion.9), channel_id=1, source_target_pairs={{0,4},{1,5},{2,6},{3,7},{8,12},{9,13},{10,14},{11,15},{16,20},{17,... | collective-permute-start | bytes 147464 | tf_op jit(solution)/shard_map/ppermute | solution.py:717
  134.3 1.7 collective-permute-done.7
  136.6 41.8 %ffn.3 = (f32[6,256,512]{2,1,0:T(8,128)}, f32[6,3,512]{2,1,0:T(4,128)}, f32[6,256,512]{2,1,0:T(8,128)}, bf16[1536,1024]{1,0:T(8,128)(2,1)}, bf16[1536,1024]{1,0:...) custom-call(f32[6,256,512]{2,1,0:T(8,128)} %get-tuple-element.113.refs_0_.refs_5_, ...), custom_call_target="tpu_custom_call" | custom-call | flops 24159191040 | bytes 65519616 | tf_op jit(solution)/shard_map/ffn/pallas_call | solution.py:695
  179.1 54.7 %ffn_back.2 = (f32[6,256,512]{2,1,0:T(8,128)}, f32[8,512]{1,0:T(8,128)}, f32[4,4,2,128,128]{4,3,2,1,0:T(8,128)}, f32[4,4,2,128,128]{4,3,2,1,0:T(8,128)}, f32[4,4...) custom-call(s32[1]{0:T(128)} %bitcast.15.refs_0_.mine_ref.refs_1_, f32[6,256,512]{2,1,0:T(8,128)} %bitcast.200, ...), custom_call_target="tpu_custom_call" | custom-call | flops 38654705664 | bytes 50429956 | tf_op jit(solution)/shard_map/ffn_back/pallas_call | solution.py:695
  234.4 11.7 %out_back.2 = (f32[6,256,1024]{2,1,0:T(8,128)}, f32[6,16,1024]{2,1,0:T(8,128)}, f32[2,6,1024]{2,1,0:T(8,128)S(1)}, bf16[512,1536]{1,0:T(8,128)(2,1)}, bf16[512,1536]{1,0:T(8,128)(2,1)}) custom-call(f32[6,256,512]{2,1,0:T(8,128)} %get-tuple-element.124.refs_0_.refs_7_, f32[6,256,8]{2,1,0:T(8,128)S(1)} %copy-done.15, ...), custom_call_target="tpu_custom_call" | custom-call | flops 4831838208 | bytes 23560192 | tf_op jit(solution)/shard_map/out_back/pallas_call | solution.py:695
  248.7 9.4 %out_grad.2 = (f32[4,4,1,128,128]{4,3,2,1,0:T(8,128)}, f32[4,4,1,128,128]{4,3,2,1,0:T(8,128)}) custom-call(s32[1]{0:T(128)} %bitcast.15.refs_0_.mine_ref.refs_1_, bf16[512,1536]{1,0:T(8,128)(2,1)} %get-tuple-element.125.gth_ref, bf16[512,1536]{1,0:T(8,128)(2,1)} %get-tuple-element.126.gtl_ref, bf16[1536,1024]{1,0:T(8,128)(2,1)} %get-tuple-element.127.sth_ref.refs_5_, ...), custom_call_target="tpu_custom_call" | custom-call | flops 4831838208 | bytes 11534340 | tf_op jit(solution)/shard_map/out_grad/pallas_call | solution.py:695
  259.7 2.5 neighbour_sum.4.refs_0_
  262.3 2.0 copy-done.1
  266.4 6.4 %collective-permute-done.12 = f32[2,6,1024]{2,1,0:T(8,128)S(1)} collective-permute-done((f32[2,6,1024]{2,1,0:T(8,128)S(1)}, f32[2,6,1024]{2,1,0:T(8,128)S(1)}, u32[]{:S(2)}, u32[]{:S(2)}) %collective-permute-start.12) | collective-permute-done | bytes 49184 | tf_op jit(solution)/shard_map/ppermute | solution.py:717
  272.8 23.8 %gates_back.2 = (bf16[1536,1024]{1,0:T(8,128)(2,1)}, bf16[1536,1024]{1,0:T(8,128)(2,1)}, bf16[1536,1024]{1,0:T(8,128)(2,1)}, bf16[1536,1024]{1,0:T(8,128)(2,1)},...) custom-call(f32[4,4,512,128]{3,2,1,0:T(8,128)} %copy-done.1, ...), custom_call_target="tpu_custom_call" | custom-call | flops 9663676416 | bytes 49807364 | tf_op jit(solution)/shard_map/gates_back/pallas_call | solution.py:695
  297.2 18.6 %conv_back.2 = (f32[6,256,512]{2,1,0:T(8,128)}, f32[6,3,512]{2,1,0:T(4,128)S(1)}, f32[32,512]{1,0:T(8,128)S(1)}) custom-call(bf16[1536,1024]{1,0:T(8,128)(2,1)} %get-tuple-element.140.refs_0_, bf16[1536,1024]{1,0:T(8,128)(2,1)} %get-tuple-element.141.refs_1_, bf16[1536,1024]{1,0:T(8,128)(2,1)} %get-tuple-element.142.refs_2_, ...), custom_call_target="tpu_custom_call" | custom-call | flops 9663676416 | bytes 30609408 | tf_op jit(solution)/shard_map/conv_back/pallas_call | solution.py:695
  315.9 2.2 neighbour_sum.5
  319.5 1.8 collective-permute-done.13.refs_2_
  321.9 53.8 %ffn_back.3 = (f32[6,256,512]{2,1,0:T(8,128)}, f32[8,512]{1,0:T(8,128)}, f32[4,4,2,128,128]{4,3,2,1,0:T(8,128)}, f32[4,4,2,128,128]{4,3,2,1,0:T(8,128)}, f32[4,4...) custom-call(s32[1]{0:T(128)} %bitcast.15.refs_0_.mine_ref.refs_1_, ...), custom_call_target="tpu_custom_call" | custom-call | flops 38654705664 | bytes 50429956 | tf_op jit(solution)/shard_map/ffn_back/pallas_call | solution.py:695
  375.7 2.9 collective-permute-start.16
  383.3 11.9 %out_back.3 = (f32[6,256,1024]{2,1,0:T(8,128)}, f32[6,16,1024]{2,1,0:T(8,128)}, f32[2,6,1024]{2,1,0:T(8,128)S(1)}, bf16[512,1536]{1,0:T(8,128)(2,1)}, bf16[512,1536]{1,0:T(8,128)(2,1)}) custom-call(f32[2,896,128]{2,1,0:T(8,128)} %get-tuple-element.153.refs_0_, f32[6,256,512]{2,1,0:T(8,128)} %get-tuple-element.150.refs_0_.refs_1_.refs_8_, ...), custom_call_target="tpu_custom_call" | custom-call | flops 4831838208 | bytes 24477696 | tf_op jit(solution)/shard_map/out_back/pallas_call | solution.py:695
  395.2 2.5 neighbour_sum.6.refs_0_
  397.7 2.0 copy-done
  399.8 1.8 collective-permute-start.20
  404.2 9.9 %out_grad.3 = (f32[4,4,1,128,128]{4,3,2,1,0:T(8,128)}, f32[4,4,1,128,128]{4,3,2,1,0:T(8,128)}) custom-call(s32[1]{0:T(128)} %bitcast.15.refs_0_.mine_ref.refs_1_, bf16[512,1536]{1,0:T(8,128)(2,1)} %get-tuple-element.154.gth_ref, bf16[512,1536]{1,0:T(8,128)(2,1)} %get-tuple-element.155.gtl_ref, bf16[1536,1024]{1,0:T(8,128)(2,1)} %get-tuple-element.156.sth_ref.refs_5_, ...), custom_call_target="tpu_custom_call" | custom-call | flops 4831838208 | bytes 11534340 | tf_op jit(solution)/shard_map/out_grad/pallas_call | solution.py:695
  414.1 10.1 %collective-permute-done.19.refs_3_ = f32[2,6,1024]{2,1,0:T(8,128)S(1)} collective-permute-done((f32[2,6,1024]{2,1,0:T(8,128)S(1)}, f32[2,6,1024]{2,1,0:T(8,128)S(1)}, u32[]{:S(2)}, u32[]{:S(2)}) %collective-permute-start.19) | collective-permute-done | bytes 49184 | tf_op jit(solution)/shard_map/ppermute | solution.py:717
  425.6 5.9 %collective-permute-done.21 = f32[2,6,1024]{2,1,0:T(8,128)S(1)} collective-permute-done((f32[2,6,1024]{2,1,0:T(8,128)S(1)}, f32[2,6,1024]{2,1,0:T(8,128)S(1)}, u32[]{:S(2)}, u32[]{:S(2)}) %collective-permute-start.21) | collective-permute-done | bytes 49184 | tf_op jit(solution)/shard_map/ppermute | solution.py:717
  433.3 23.4 %gates_back.3 = (bf16[1536,1024]{1,0:T(8,128)(2,1)}, bf16[1536,1024]{1,0:T(8,128)(2,1)}, bf16[1536,1024]{1,0:T(8,128)(2,1)}, bf16[1536,1024]{1,0:T(8,128)(2,1)},...) custom-call(f32[1,896,128]{2,1,0:T(8,128)} %copy-done.40, ...), custom_call_target="tpu_custom_call" | custom-call | flops 9663676416 | bytes 46071812 | tf_op jit(solution)/shard_map/gates_back/pallas_call | solution.py:695
  460.7 2.2 collective-permute-done.22.refs_2_
  464.7 4.1 neighbour_sum.7.refs_0_
  470.4 23.3 %conv_back.3 = (f32[6,256,512]{2,1,0:T(8,128)}, f32[6,3,512]{2,1,0:T(4,128)S(1)}, f32[32,512]{1,0:T(8,128)S(1)}) custom-call(f32[4,4,384,128]{3,2,1,0:T(8,128)} %neighbour_sum.7.refs_0_, bf16[1536,1024]{1,0:T(8,128)(2,1)} %get-tuple-element.175.refs_1_, bf16[1536,1024]{1,0:T(8,128)(2,1)} %get-tuple-element.176.refs_2_, ...), custom_call_target="tpu_custom_call" | custom-call | flops 9663676416 | bytes 33755136 | tf_op jit(solution)/shard_map/conv_back/pallas_call | solution.py:695
  495.0 1.8 collective-permute-start.26
  499.0 3.2 collective-permute-start.27
  505.9 3.3 collective-permute-done.28
  513.3 2.5 collective-permute-start.34
  517.0 1.9 collective-permute-start.30
  521.3 5.3 collective-permute-done.34.refs_3_
  526.6 3.4 collective-permute-done.30.refs_2_
  530.1 1.6 collective-permute-start.31
  532.7 6.8 %collective-permute-done.31.refs_2_ = f32[1,384,128]{2,1,0:T(8,128)S(1)} collective-permute-done((f32[1,384,128]{2,1,0:T(8,128)S(1)}, f32[1,384,128]{2,1,0:T(8,128)S(1)}, u32[]{:S(2)}, u32[]{:S(2)}) %collective-permute-start.31) | collective-permute-done | bytes 196640 | tf_op jit(solution)/shard_map/ppermute | solution.py:721
  (234 shorter events, 53.9 us)
Async XLA Ops:
  7.2 371.5 %reduce-scatter.13.cloned.1.call-start = ((), (), s32[]{:S(2)}) async-start(), calls=%async_computation.4 | async-start | bytes 5242880
  8.8 4.4 collective-permute-start
  12.4 26.3 %copy-start.13 = (f32[6,256,8]{2,1,0:T(8,128)}, f32[6,256,8]{2,1,0:T(8,128)S(1)}, u32[]{:S(2)}) copy-start(f32[6,256,8]{2,1,0:T(8,128)S(1)} %fusion.refs_2_.refs_1_.refs_7_.refs_4_.refs_5_) | copy-start | bytes 147460
  13.2 25.5 %copy-start.38 = (f32[4,512]{1,0:T(4,128)}, f32[4,512]{1,0:T(4,128)S(1)}, u32[]{:S(2)}) copy-start(f32[4,512]{1,0:T(4,128)S(1)} %get-tuple-element.234.refs_4_.refs_9_) | copy-start | bytes 24580
  13.2 25.5 %copy-start.42 = (f32[6,3,512]{2,1,0:T(4,128)}, f32[6,3,512]{2,1,0:T(4,128)S(1)}, u32[]{:S(2)}) copy-start(f32[6,3,512]{2,1,0:T(4,128)S(1)} %collective-permute-done.refs_1_.refs_7_) | copy-start | bytes 110596
  38.7 3.6 collective-permute-start.1
  42.3 5.5 %collective-permute-start.2 = (f32[2,6,1024]{2,1,0:T(8,128)S(1)}, f32[2,6,1024]{2,1,0:T(8,128)S(1)}, u32[]{:S(2)}, u32[]{:S(2)}) collective-permute-start(f32[2,6,1024]{2,1,0:T(8,128)S(1)} %fusion.2), channel_id=1, source_target_pairs={{0,2},{1,3},{2,4},{3,5},{4,6},{5,7},{8,10},{9,11},{10,12},{11,13},... | collective-permute-start | bytes 147464 | tf_op jit(solution)/shard_map/ppermute | solution.py:717
  47.9 7.2 %collective-permute-start.3 = (f32[2,6,1024]{2,1,0:T(8,128)S(1)}, f32[2,6,1024]{2,1,0:T(8,128)S(1)}, u32[]{:S(2)}, u32[]{:S(2)}) collective-permute-start(f32[2,6,1024]{2,1,0:T(8,128)S(1)} %pad_maximum_fusion.8), channel_id=1, source_target_pairs={{0,4},{1,5},{2,6},{3,7},{8,12},{9,13},{10,14},{11,15},{16,20},{17,... | collective-permute-start | bytes 147464 | tf_op jit(solution)/shard_map/ppermute | solution.py:717
  55.7 41.3 %copy-start.14 = (f32[6,256,8]{2,1,0:T(8,128)S(1)}, f32[6,256,8]{2,1,0:T(8,128)}, u32[]{:S(2)}) copy-start(f32[6,256,8]{2,1,0:T(8,128)} %copy-done.13) | copy-start | bytes 147460
  55.7 41.3 %copy-start.35 = (f32[2,512]{1,0:T(2,128)S(1)}, f32[2,512]{1,0:T(2,128)}, u32[]{:S(2)}) copy-start(f32[2,512]{1,0:T(2,128)} %refs_10_.7) | copy-start | bytes 12292
  94.6 2.4 collective-permute-start.4
  118.2 4.1 collective-permute-start.5
  122.3 6.3 %collective-permute-start.6 = (f32[2,6,1024]{2,1,0:T(8,128)S(1)}, f32[2,6,1024]{2,1,0:T(8,128)S(1)}, u32[]{:S(2)}, u32[]{:S(2)}) collective-permute-start(f32[2,6,1024]{2,1,0:T(8,128)S(1)} %fusion.1), channel_id=1, source_target_pairs={{0,2},{1,3},{2,4},{3,5},{4,6},{5,7},{8,10},{9,11},{10,12},{11,13},... | collective-permute-start | bytes 147464 | tf_op jit(solution)/shard_map/ppermute | solution.py:717
  128.6 7.5 %collective-permute-start.7 = (f32[2,6,1024]{2,1,0:T(8,128)S(1)}, f32[2,6,1024]{2,1,0:T(8,128)S(1)}, u32[]{:S(2)}, u32[]{:S(2)}) collective-permute-start(f32[2,6,1024]{2,1,0:T(8,128)S(1)} %pad_maximum_fusion.9), channel_id=1, source_target_pairs={{0,4},{1,5},{2,6},{3,7},{8,12},{9,13},{10,14},{11,15},{16,20},{17,... | collective-permute-start | bytes 147464 | tf_op jit(solution)/shard_map/ppermute | solution.py:717
  179.1 55.3 %copy-start.15 = (f32[6,256,8]{2,1,0:T(8,128)S(1)}, f32[6,256,8]{2,1,0:T(8,128)}, u32[]{:S(2)}) copy-start(f32[6,256,8]{2,1,0:T(8,128)} %copy-done.13) | copy-start | bytes 147460
  233.8 24.9 %collective-permute-start.10 = (f32[4,4,256,128]{3,2,1,0:T(8,128)}, f32[4,4,256,128]{3,2,1,0:T(8,128)S(1)}, u32[]{:S(2)}, u32[]{:S(2)}) collective-permute-start(f32[4,4,256,128]{3,2,1,0:T(8,128)} %bitcast.204), channel_id=1, source_target_pairs={{0,1},{1,0},{2,3},{3,2},{4,5},{5,4},{6,7},{7,6},{8,9},{9,8},{10,11... | collective-permute-start | bytes 6291464 | tf_op jit(solution)/shard_map/ppermute | solution.py:721
  233.9 24.9 %collective-permute-start.11 = (f32[4,4,256,128]{3,2,1,0:T(8,128)}, f32[4,4,256,128]{3,2,1,0:T(8,128)}, u32[]{:S(2)}, u32[]{:S(2)}) collective-permute-start(f32[4,4,256,128]{3,2,1,0:T(8,128)} %bitcast.203), channel_id=1, source_target_pairs={{0,1},{1,0},{2,3},{3,2},{4,5},{5,4},{6,7},{7,6},{8,9},{9,8},{10,11... | collective-permute-start | bytes 6291464 | tf_op jit(solution)/shard_map/ppermute | solution.py:721
  246.1 1.3 collective-permute-start.8
  247.4 10.7 %collective-permute-start.9 = (f32[2,6,1024]{2,1,0:T(8,128)S(1)}, f32[2,6,1024]{2,1,0:T(8,128)S(1)}, u32[]{:S(2)}, u32[]{:S(2)}) collective-permute-start(f32[2,6,1024]{2,1,0:T(8,128)S(1)} %carry.4.refs_4_), channel_id=1, source_target_pairs={{2,0},{3,1},{4,2},{5,3},{6,4},{7,5},{10,8},{11,9},{12,10},{13,11},... | collective-permute-start | bytes 147464 | tf_op jit(solution)/shard_map/ppermute | solution.py:717
  264.3 114.4 %reduce-scatter.15.cloned.1.call-start = ((), (), s32[]{:S(2)}) async-start(), calls=%async_computation.5 | async-start | bytes 3932160
  265.1 7.7 %collective-permute-start.12 = (f32[2,6,1024]{2,1,0:T(8,128)S(1)}, f32[2,6,1024]{2,1,0:T(8,128)S(1)}, u32[]{:S(2)}, u32[]{:S(2)}) collective-permute-start(f32[2,6,1024]{2,1,0:T(8,128)S(1)} %copy-done.28), channel_id=1, source_target_pairs={{4,0},{5,1},{6,2},{7,3},{12,8},{13,9},{14,10},{15,11},{20,16},{21,... | collective-permute-start | bytes 147464 | tf_op jit(solution)/shard_map/ppermute | solution.py:717
  272.8 24.4 %copy-start.36 = (f32[2,512]{1,0:T(2,128)S(1)}, f32[2,512]{1,0:T(2,128)}, u32[]{:S(2)}) copy-start(f32[2,512]{1,0:T(2,128)} %refs_10_.7) | copy-start | bytes 12292
  296.6 19.2 %collective-permute-start.15 = (f32[4,4,256,128]{3,2,1,0:T(8,128)}, f32[4,4,256,128]{3,2,1,0:T(8,128)S(1)}, u32[]{:S(2)}, u32[]{:S(2)}) collective-permute-start(f32[4,4,256,128]{3,2,1,0:T(8,128)} %bitcast.206), channel_id=1, source_target_pairs={{0,1},{1,0},{2,3},{3,2},{4,5},{5,4},{6,7},{7,6},{8,9},{9,8},{10,11... | collective-permute-start | bytes 6291464 | tf_op jit(solution)/shard_map/ppermute | solution.py:721
  296.7 19.1 %collective-permute-start.14 = (f32[4,4,128,128]{3,2,1,0:T(8,128)S(1)}, f32[4,4,128,128]{3,2,1,0:T(8,128)S(1)}, u32[]{:S(2)}, u32[]{:S(2)}) collective-permute-start(f32[4,4,128,128]{3,2,1,0:T(8,128)S(1)} %bitcast.179), channel_id=1, source_target_pairs={{0,1},{1,0},{2,3},{3,2},{4,5},{5,4},{6,7},{7,6},{8,9},{9,8},{10,11... | collective-permute-start | bytes 3145736 | tf_op jit(solution)/shard_map/ppermute | solution.py:721
  318.1 139.6 %reduce-scatter.17.cloned.1.call-start = ((), (), s32[]{:S(2)}) async-start(), calls=%async_computation.6 | async-start | bytes 5242880
  318.2 3.1 collective-permute-start.13
  375.7 19.4 %collective-permute-start.16 = (f32[4,4,256,128]{3,2,1,0:T(8,128)}, f32[4,4,256,128]{3,2,1,0:T(8,128)S(1)}, u32[]{:S(2)}, u32[]{:S(2)}) collective-permute-start(f32[4,4,256,128]{3,2,1,0:T(8,128)} %bitcast.202), channel_id=1, source_target_pairs={{0,1},{1,0},{2,3},{3,2},{4,5},{5,4},{6,7},{7,6},{8,9},{9,8},{10,11... | collective-permute-start | bytes 6291464 | tf_op jit(solution)/shard_map/ppermute | solution.py:721
  378.6 16.6 %collective-permute-start.17 = (f32[4,4,256,128]{3,2,1,0:T(8,128)}, f32[4,4,256,128]{3,2,1,0:T(8,128)}, u32[]{:S(2)}, u32[]{:S(2)}) collective-permute-start(f32[4,4,256,128]{3,2,1,0:T(8,128)} %bitcast.201), channel_id=1, source_target_pairs={{0,1},{1,0},{2,3},{3,2},{4,5},{5,4},{6,7},{7,6},{8,9},{9,8},{10,11... | collective-permute-start | bytes 6291464 | tf_op jit(solution)/shard_map/ppermute | solution.py:721
  399.8 116.0 %reduce-scatter.19.cloned.1.call-start = ((), (), s32[]{:S(2)}) async-start(), calls=%async_computation.7 | async-start | bytes 3932160
  399.8 31.7 %collective-permute-start.20 = (f32[2,896,128]{2,1,0:T(8,128)}, f32[2,896,128]{2,1,0:T(8,128)S(1)}, u32[]{:S(2)}, u32[]{:S(2)}) collective-permute-start(f32[2,896,128]{2,1,0:T(8,128)} %get-tuple-element.153.refs_0_), channel_id=1, source_target_pairs={{0,2},{1,3},{2,0},{3,1},{4,6},{5,7},{6,4},{7,5},{8,10},{9,11},{10,... | collective-permute-start | bytes 2752520 | tf_op jit(solution)/shard_map/ppermute | solution.py:721
  401.6 1.3 collective-permute-start.18
  402.9 21.3 %collective-permute-start.19 = (f32[2,6,1024]{2,1,0:T(8,128)S(1)}, f32[2,6,1024]{2,1,0:T(8,128)S(1)}, u32[]{:S(2)}, u32[]{:S(2)}) collective-permute-start(f32[2,6,1024]{2,1,0:T(8,128)S(1)} %carry.6.refs_4_), channel_id=1, source_target_pairs={{2,0},{3,1},{4,2},{5,3},{6,4},{7,5},{10,8},{11,9},{12,10},{13,11},... | collective-permute-start | bytes 147464 | tf_op jit(solution)/shard_map/ppermute | solution.py:717
  424.2 7.3 %collective-permute-start.21 = (f32[2,6,1024]{2,1,0:T(8,128)S(1)}, f32[2,6,1024]{2,1,0:T(8,128)S(1)}, u32[]{:S(2)}, u32[]{:S(2)}) collective-permute-start(f32[2,6,1024]{2,1,0:T(8,128)S(1)} %carry.7.refs_0_), channel_id=1, source_target_pairs={{4,0},{5,1},{6,2},{7,3},{12,8},{13,9},{14,10},{15,11},{20,16},{21,... | collective-permute-start | bytes 147464 | tf_op jit(solution)/shard_map/ppermute | solution.py:717
  433.3 29.9 %copy-start.2 = (f32[4,4,1,128,128]{4,3,2,1,0:T(8,128)S(1)}, f32[4,4,1,128,128]{4,3,2,1,0:T(8,128)}, u32[]{:S(2)}) copy-start(f32[4,4,1,128,128]{4,3,2,1,0:T(8,128)} %get-tuple-element.158.refs_0_) | copy-start | bytes 3145732
  457.3 5.9 %collective-permute-start.23 = (f32[4,4,256,128]{3,2,1,0:T(8,128)}, f32[4,4,256,128]{3,2,1,0:T(8,128)S(1)}, u32[]{:S(2)}, u32[]{:S(2)}) collective-permute-start(f32[4,4,256,128]{3,2,1,0:T(8,128)} %bitcast.205), channel_id=1, source_target_pairs={{0,1},{1,0},{2,3},{3,2},{4,5},{5,4},{6,7},{7,6},{8,9},{9,8},{10,11... | collective-permute-start | bytes 6291464 | tf_op jit(solution)/shard_map/ppermute | solution.py:721
  457.3 5.6 %collective-permute-start.22 = (f32[4,4,128,128]{3,2,1,0:T(8,128)}, f32[4,4,128,128]{3,2,1,0:T(8,128)}, u32[]{:S(2)}, u32[]{:S(2)}) collective-permute-start(f32[4,4,128,128]{3,2,1,0:T(8,128)} %bitcast.43), channel_id=1, source_target_pairs={{0,1},{1,0},{2,3},{3,2},{4,5},{5,4},{6,7},{7,6},{8,9},{9,8},{10,11... | collective-permute-start | bytes 3145736 | tf_op jit(solution)/shard_map/ppermute | solution.py:721
  469.9 23.9 %collective-permute-start.32 = (f32[1,896,128]{2,1,0:T(8,128)S(1)}, f32[1,896,128]{2,1,0:T(8,128)S(1)}, u32[]{:S(2)}, u32[]{:S(2)}) collective-permute-start(f32[1,896,128]{2,1,0:T(8,128)S(1)} %copy-done.41), channel_id=1, source_target_pairs={{0,4},{1,5},{2,6},{3,7},{4,0},{5,1},{6,2},{7,3},{8,12},{9,13},{10,... | collective-permute-start | bytes 1376264 | tf_op jit(solution)/shard_map/ppermute | solution.py:721
  470.1 43.1 %collective-permute-start.33 = (f32[2,512,128]{2,1,0:T(8,128)S(1)}, f32[2,512,128]{2,1,0:T(8,128)S(1)}, u32[]{:S(2)}, u32[]{:S(2)}) collective-permute-start(f32[2,512,128]{2,1,0:T(8,128)S(1)} %copy-done.22), channel_id=1, source_target_pairs={{0,2},{1,3},{2,0},{3,1},{4,6},{5,7},{6,4},{7,5},{8,10},{9,11},{10,... | collective-permute-start | bytes 1572872 | tf_op jit(solution)/shard_map/ppermute | solution.py:721
  493.7 1.3 collective-permute-start.25
  493.9 26.2 %copy-start.46 = (f32[2,512,4]{1,2,0:T(4,128)S(1)}, f32[2,512,4]{1,2,0:T(4,128)}, u32[]{:S(2)}) copy-start(f32[2,512,4]{1,2,0:T(4,128)} %param.16) | copy-start | bytes 49156
  495.0 4.0 collective-permute-start.26
  496.8 5.4 collective-permute-start.24
  499.0 5.6 %collective-permute-start.27 = (f32[2,7,512]{2,1,0:T(8,128)S(1)}, f32[2,7,512]{2,1,0:T(8,128)S(1)}, u32[]{:S(2)}, u32[]{:S(2)}) collective-permute-start(f32[2,7,512]{2,1,0:T(8,128)S(1)} %fusion.23), channel_id=1, source_target_pairs={{0,4},{1,5},{2,6},{3,7},{4,0},{5,1},{6,2},{7,3},{8,12},{9,13},{10,... | collective-permute-start | bytes 86024 | tf_op jit(solution)/shard_map/ppermute | solution.py:840
  504.6 4.6 collective-permute-start.28
  509.2 3.9 collective-permute-start.29
  513.3 13.3 %collective-permute-start.34 = (f32[1,512,128]{2,1,0:T(8,128)S(1)}, f32[1,512,128]{2,1,0:T(8,128)S(1)}, u32[]{:S(2)}, u32[]{:S(2)}) collective-permute-start(f32[1,512,128]{2,1,0:T(8,128)S(1)} %get-tuple-element.193), channel_id=1, source_target_pairs={{0,4},{1,5},{2,6},{3,7},{4,0},{5,1},{6,2},{7,3},{8,12},{9,13},{10,... | collective-permute-start | bytes 786440 | tf_op jit(solution)/shard_map/ppermute | solution.py:721
  517.0 13.0 %collective-permute-start.30 = (f32[2,384,128]{2,1,0:T(8,128)S(1)}, f32[2,384,128]{2,1,0:T(8,128)S(1)}, u32[]{:S(2)}, u32[]{:S(2)}) collective-permute-start(f32[2,384,128]{2,1,0:T(8,128)S(1)} %get-tuple-element.187), channel_id=1, source_target_pairs={{0,2},{1,3},{2,0},{3,1},{4,6},{5,7},{6,4},{7,5},{8,10},{9,11},{10,... | collective-permute-start | bytes 1179656 | tf_op jit(solution)/shard_map/ppermute | solution.py:721
  530.1 9.4 %collective-permute-start.31 = (f32[1,384,128]{2,1,0:T(8,128)S(1)}, f32[1,384,128]{2,1,0:T(8,128)S(1)}, u32[]{:S(2)}, u32[]{:S(2)}) collective-permute-start(f32[1,384,128]{2,1,0:T(8,128)S(1)} %get-tuple-element.189), channel_id=1, source_target_pairs={{0,4},{1,5},{2,6},{3,7},{4,0},{5,1},{6,2},{7,3},{8,12},{9,13},{10,... | collective-permute-start | bytes 589832 | tf_op jit(solution)/shard_map/ppermute | solution.py:721
  (42 other events, 227.8 us)
Sparse Core Ops, SparseCore 0:
  264.4 55.6 reduce-scatter.12
  324.0 43.9 reduce-scatter.14
  399.9 52.0 reduce-scatter.16
  469.1 42.4 reduce-scatter.18

commit v2 on v1

--- a/solution.py
+++ b/solution.py
@@ -69,31 +69,37 @@
     return jnp.concatenate([high_ref[...], low_ref[...], high_ref[...]], 1)
 
 
-def load_rows(ref, b, tmp, put):
+def turn_eight(values):
+    row = lax.broadcasted_iota(jnp.int32, values[0].shape, 0)
+    for d in (4, 2, 1):
+        low = (row & d) == 0
+        out = list(values)
+        for a in range(8):
+            if a & d == 0:
+                first, second = values[a], values[a + d]
+                out[a] = jnp.where(low, first, pltpu.roll(second, d, 0))
+                out[a + d] = jnp.where(low, pltpu.roll(first, 8 - d, 0), second)
+        values = out
+    return values
+
+
+def load_rows(ref, b, natural, put):
     size = ref.shape[1]
-    if tmp is not None:
-        for k in range(tmp.shape[0]):
-            tmp[k] = ref[b, :, 128 * k : 128 * (k + 1)]
-    for r in range(0, size, 16):
-        if tmp is None:
-            put(r, ref[b, r : r + 16, :])
-        else:
-            groups = [
-                jnp.concatenate([tmp[k, pl.ds(i, 8, stride=size // 8), :] for k in range(tmp.shape[0])], 1)
-                for i in (r // 8, r // 8 + 1)
-            ]
-            put(r, jnp.concatenate(groups, 0))
-
-
-def store_rows(ref, b, values, tmp):
-    if tmp is None:
-        ref[b] = values
+    if not natural:
+        for r in range(0, size, 8):
+            put(r, ref[b, r : r + 8, :])
         return
-    rows = ref.shape[1] // 8
-    for k in range(tmp.shape[0]):
-        for i in range(rows):
-            tmp[k, pl.ds(i, 8, stride=rows), :] = values[i * 8 : (i + 1) * 8, 128 * k : 128 * (k + 1)]
-        ref[b, :, 128 * k : 128 * (k + 1)] = tmp[k]
+    long = size // 8
+    for m in range(0, long, 8):
+        for i, value in enumerate(turn_eight([ref[b, c * long + m : c * long + m + 8, :] for c in range(8)])):
+            put(8 * (m + i), value)
+
+
+def store_rows(ref, b, get):
+    long = ref.shape[1] // 8
+    for m in range(0, long, 8):
+        for c, value in enumerate(turn_eight([get(8 * (m + i)) for i in range(8)])):
+            ref[b, c * long + m : c * long + m + 8, :] = value
 
 
 def inverse_rms(values):
@@ -163,7 +169,6 @@
     rest = list(refs[14:])
     xp_ref = rest.pop(0) if natural else None
     cat_ref, right_ref, ext_ref = rest[:3]
-    tmp = rest[3] if natural else None
     batch, size, width = x_ref.shape
     step = sg_ref.shape[-1]
     head = 8 * (taps_ref.shape[0] - 1)
@@ -174,10 +179,10 @@
         def prepare(b, _):
             def put(r, x):
                 if natural:
-                    xp_ref[b, r : r + 16, :] = x
-                ext_ref[head + r : head + r + 16, :] = x * inverse_rms(x) * gain
-
-            load_rows(x_ref, b, tmp, put)
+                    xp_ref[b, r : r + 8, :] = x
+                ext_ref[head + r : head + r + 8, :] = x * inverse_rms(x) * gain
+
+            load_rows(x_ref, b, natural, put)
             edge = edge_ref[b]
             extend(ext_ref, edge * inverse_rms(edge) * gain)
             for r in range(0, size, 16):
@@ -231,7 +236,7 @@
     x_ref, m_ref, sg_ref, sp_ref, eq_ref, inc_ref, wo_ref, gain_ref, up_ref, dn_ref = refs[:10]
     y_ref, last_ref, mid_ref, sth_ref, stl_ref, pre_ref, nth_ref, ntl_ref = refs[10:18]
     cat_ref, ro_ref, ru_ref, rd_ref, act_ref = refs[18:23]
-    tmp = refs[23] if natural else None
+    acc_ref = refs[23] if natural else y_ref
     batch, size, width = x_ref.shape
     n = pl.program_id(0)
 
@@ -265,7 +270,7 @@
         def prepare(b, _):
             for r in range(0, size, 16):
                 middle = mid_ref[b, r : r + 16, :]
-                y_ref[b, r : r + 16, :] = middle
+                acc_ref[b, r : r + 16, :] = middle
                 rows = pl.ds(pl.multiple_of(b * size + r, 16), 16)
                 put_left(cat_ref, middle * inverse_rms(middle) * gain, rows)
             return _
@@ -293,7 +298,7 @@
                 pre_ref[b * size + r : b * size + r + 16, :] = pre
                 put_left(act, pre * gelu_parts(pre)[2], slice(r, r + 16))
             turn_slice(cat_ref, b, size, n - first_steps, nth_ref, ntl_ref)
-            y_ref[b] += dot(act[...], rd_ref[...])
+            acc_ref[b] += dot(act[...], rd_ref[...])
 
     @pl.when(n == pl.num_programs(0) - 1)
     def _():
@@ -302,9 +307,9 @@
         def finish(b, _):
             for k in range(count):
                 row = size - 8 * (count - k) + 7
-                last_ref[b, k : k + 1, :] = y_ref[b, row : row + 1, :]
+                last_ref[b, k : k + 1, :] = acc_ref[b, row : row + 1, :]
             if natural:
-                store_rows(y_ref, b, y_ref[b], tmp)
+                store_rows(y_ref, b, lambda r: acc_ref[b, r : r + 8, :])
             return _
 
         lax.fori_loop(0, batch, finish, 0)
@@ -343,12 +348,12 @@
     return jnp.concatenate([high_ref[...], high_ref[...], low_ref[...]], 0)
 
 
-def ffn_back_kernel(natural, layer, plans, *refs):
+def ffn_back_kernel(natural, layer, plans, afters, *refs):
+    refs = refs[afters:]
     mine_ref, gy_ref, got_ref, last_ref, first_ref, mid_hbm, gain_ref, nth_hbm, ntl_hbm, pre_ref, dn_ref, up_ref = refs[:12]
     gm_ref, sec_ref, dk_ref, ds_ref, uk_ref, us_ref = refs[12:18]
     cat_ref, gyt_ref, ah_ref, al_ref, gh_ref, gl_ref, rd_ref, ru_ref, gn_ref = refs[18:27]
     mid_ref, nth_ref, ntl_ref, sems = refs[27:31]
-    tmp = refs[31] if natural else None
     batch, size, width = gy_ref.shape
     n = pl.program_id(0)
     mine = mine_ref[0]
@@ -365,9 +370,9 @@
             start = pl.multiple_of(b * size, size)
 
             def put(r, gy):
-                gm_ref[b, r : r + 16, :] = gy
-
-            load_rows(gy_ref, b, tmp, put)
+                gm_ref[b, r : r + 8, :] = gy
+
+            load_rows(gy_ref, b, natural, put)
             if not natural:
                 count = last_ref.shape[1]
                 at = lax.broadcasted_iota(jnp.int32, (8, width), 0) == 7
@@ -480,7 +485,9 @@
     pl.when(n != 0)(lambda: body(False, False))
 
 
-def out_grad_kernel(plan, mine_ref, gth_ref, gtl_ref, sth_ref, stl_ref, ok_ref, os_ref):
+def out_grad_kernel(plan, afters, *refs):
+    mine_ref, gth_ref, gtl_ref, sth_ref, stl_ref = refs[afters : afters + 5]
+    ok_ref, os_ref = refs[-2:]
     emit(mine_ref[0], dot(three_left(gth_ref, gtl_ref), three(sth_ref, stl_ref)), ok_ref, os_ref, plan)
 
 
@@ -537,7 +544,6 @@
     glh_ref, gll_ref, gch_ref, gcl_ref, m_ref, x_ref, edge_ref, gm_ref, taps_ref, gain_ref, w_ref = refs[:11]
     gx_ref, send_ref, s_ref = refs[11:14]
     right_ref, acc_ref, ext_ref, out_ref = refs[14:18]
-    tmp = refs[18] if natural else None
     _, size, width = x_ref.shape
     taps = taps_ref.shape[0]
     head = 8 * (taps - 1)
@@ -593,7 +599,7 @@
         for j in range(taps):
             s_ref[8 * j : 8 * (j + 1)] = sums[j]
         if natural:
-            store_rows(gx_ref, 0, out_ref[...], tmp)
+            store_rows(gx_ref, 0, lambda r: out_ref[r : r + 8, :])
 
     @pl.when(n == 0)
     def _():
@@ -679,7 +685,7 @@
     return min(total, VMEM)
 
 
-def call(kernel, grid, ins, outs, scratch=(), flops=0, name=None, free=False):
+def call(kernel, grid, ins, outs, scratch=(), flops=0, name=None, free=False, aliases=()):
     def large(array):
         return math.prod(array.shape) * array.dtype.itemsize > LARGE
 
@@ -704,6 +710,7 @@
         ),
         cost_estimate=pl.CostEstimate(flops=int(flops), bytes_accessed=int(moved), transcendentals=0),
         name=name,
+        input_output_aliases=dict(aliases),
     )(*args)
 
 
@@ -769,8 +776,25 @@
             else:
                 pair = combine(got, pair)
         dist *= 2
-    enters = jnp.where(is_later, other[0] * before[1] + other[1], before[1])
-    return (enters, pair) if back else enters
+    if back:
+        return functools.partial(entering_carry, is_later, other, before), pair
+    return jnp.where(is_later, other[0] * before[1] + other[1], before[1])
+
+
+def entering_carry(is_later, other, before, afters):
+    def kernel(*refs):
+        flag, other_ref, before_ref, out_ref = refs[len(afters) :]
+        further = other_ref[0] * before_ref[1] + other_ref[1]
+        out_ref[...] = jnp.where(flag[0] != 0, further, before_ref[1])
+
+    flag = (is_later.astype(jnp.int32).reshape(1), pl.BlockSpec(memory_space=pltpu.SMEM))
+    return call(
+        kernel,
+        1,
+        kept_back(afters) + [flag, fixed(other), fixed(before)],
+        [out_fixed(*other.shape[1:])],
+        name="carry",
+    )[0]
 
 
 def document_masks(starts_rows, group):
@@ -815,8 +839,10 @@
                 spec = pl.BlockSpec((halves,) + block, lambda n: (0, n // per, 0, n % per, 0, 0))
                 self.out = (shape(halves, *dims), spec)
 
-    def outs(self):
-        return [self.out, self.out if self.direct else out_fixed(8, 128)]
+    def outs(self, at=lambda n: n):
+        array, spec = self.out
+        out = (array, pl.BlockSpec(spec.block_shape, lambda n: spec.index_map(at(n))))
+        return [out, out if self.direct else out_fixed(8, 128)]
 
     def pieces(self, array):
         return array.reshape(self.rows, self.seq // 2, -1, 128)
@@ -840,6 +866,34 @@
             value = value + lax.ppermute(value, axis, [(i, i ^ flip) for i in range(size)])
             flip *= 2
     return value
+
+
+def pack_small(smalls, taps, afters):
+    layers = len(smalls)
+    width = smalls[0][0].shape[1]
+    hidden = smalls[0][2].shape[1]
+    count = hidden // width
+
+    def kernel(*refs):
+        refs = refs[len(afters) :]
+        out_ref = refs[-1]
+        for layer in range(layers):
+            sums, sec, bias = refs[3 * layer : 3 * layer + 3]
+            for j in range(taps):
+                out_ref[layer, j : j + 1, :] = jnp.sum(sums[8 * j : 8 * (j + 1)], 0, keepdims=True)
+            out_ref[layer, taps : taps + 1, :] = jnp.sum(sec[...], 0, keepdims=True)
+            for k in range(count):
+                row = jnp.sum(bias[:, k * width : (k + 1) * width], 0, keepdims=True)
+                out_ref[layer, taps + 1 + k : taps + 2 + k, :] = row
+
+    return call(
+        kernel,
+        1,
+        kept_back(afters) + [fixed(a) for group in smalls for a in group],
+        [out_fixed(layers, taps + 1 + count, width)],
+        name="pack_small",
+        free=True,
+    )[0]
 
 
 def pair_sum(parts, afters=()):
@@ -905,7 +959,6 @@
         + ([fixed(got)] if got is not None else []),
         [out_fixed(half, total, 128) for _ in range(2 if places > 1 else 1)],
         name="seq_sum",
-        free=True,
     )
 
 
@@ -948,7 +1001,6 @@
         and all(n % (128 * seq_size) == 0 and CHUNK % (2 * n // seq_size) == 0 for n in (ff, hidden))
     )
     extended = pltpu.VMEM((8 * (taps - 1) + group, width), F32)
-    order = [pltpu.VMEM((width // 128, group, 128), F32)]
     mine = (lax.axis_index("seq") % 2).astype(jnp.int32).reshape(1)
     mine = (mine, pl.BlockSpec(memory_space=pltpu.SMEM))
     masks = document_masks(starts.reshape(batch, -1), group)
@@ -978,8 +1030,7 @@
             [chunked(row_hidden), chunked(row_hidden), chunked(row_eq), chunked(row_own)]
             + [chunked(turned, axis=0, step=width // steps) for _ in range(2)]
             + ([out_fixed(batch, group, width)] if natural else []),
-            scratch=[pltpu.VMEM((tokens, 3 * width), BF), pltpu.VMEM((3 * width, 2 * CHUNK), BF), extended]
-            + (order if natural else []),
+            scratch=[pltpu.VMEM((tokens, 3 * width), BF), pltpu.VMEM((3 * width, 2 * CHUNK), BF), extended],
             flops=in_flops,
             name="gates",
         )
@@ -1021,7 +1072,7 @@
                 pltpu.VMEM((3 * CHUNK, width), BF),
                 pltpu.VMEM((2, group, 3 * CHUNK), BF),
             ]
-            + (order if final else []),
+            + ([pltpu.VMEM((batch, group, width), F32)] if final else []),
             flops=out_flops + ffn_flops,
             name="ffn",
         )
@@ -1045,10 +1096,12 @@
         final = layer == layers - 1
         first = layer == 0
         above = last_rows if final else saved[layer + 1][1]
+        waiting = [early_rows[layer + 1]] if direct and not final else []
         res = call(
-            functools.partial(ffn_back_kernel, final, layer, (down_plan.plan, up_plan.plan)),
+            functools.partial(ffn_back_kernel, final, layer, (down_plan.plan, up_plan.plan), len(waiting)),
             ff // CHUNK,
-            [mine, fixed(grad), fixed(got), fixed(above), fixed(first_gain)]
+            kept_back(waiting)
+            + [mine, fixed(grad), fixed(got), fixed(above), fixed(first_gain)]
             + [in_hbm(mid), fixed(second_gain), in_hbm(nt[0]), in_hbm(nt[1]), chunked(pre)]
             + [chunked(down_weight, axis=1, layer=layer), chunked(up_weight, layer=layer)],
             [out_fixed(batch, group, width), out_fixed(8, width)] + down_plan.outs() + up_plan.outs(),
@@ -1066,14 +1119,12 @@
                 pltpu.VMEM((width, tokens), BF),
                 pltpu.VMEM((width, tokens), BF),
                 pltpu.SemaphoreType.DMA((3,)),
-            ]
-            + (order if final else []),
+            ],
             flops=2 * ffn_flops,
             name="ffn_back",
         )
         gm, sec, down_g, up_g = res[0], res[1], res[2:4], res[4:6]
         waiting = []
-        z_next = None
         if direct and not final:
             z_next = seq_step([early_rows[layer + 1], late_rows[layer + 1]], 1, None, [gm])
             waiting = [z_next[1]]
@@ -1088,28 +1139,41 @@
             name="out_back",
         )
         gs, beq, own, gmt = res[0], res[1], res[2], res[3:5]
-        out_g = call(
-            functools.partial(out_grad_kernel, out_plan.plan),
-            hidden // CHUNK,
-            [mine, fixed(gmt[0]), fixed(gmt[1]), chunked(st[0]), chunked(st[1])],
-            out_plan.outs(),
-            flops=out_flops,
-            name="out_grad",
-        )
+
+        def out_grad(chunk, before, afters):
+            def place(n):
+                return chunk
+
+            ins = kept_back(afters) + [mine, fixed(gmt[0]), fixed(gmt[1]), chunked(st[0], place), chunked(st[1], place)]
+            outs = out_plan.outs(place)
+            return call(
+                functools.partial(out_grad_kernel, out_plan.plan, len(afters)),
+                1,
+                ins + kept_back(before),
+                outs,
+                flops=out_flops * CHUNK // hidden,
+                name="out_grad",
+                aliases=[(len(ins) + k, k) for k in range(len(before))],
+            )
+
+        out_g = out_grad(0, (), ())
         waiting = []
-        fillers = [[], list(out_g)]
+        fillers = [[], [out_g[0]]]
         if direct:
             early_parts = [tuple(down_plan.pieces(v) for v in down_g), tuple(up_plan.pieces(v) for v in up_g)]
             if first:
                 early = pair_sum(early_parts, [gs])
                 early_rows[layer] = reduce_rows(early)
                 fillers[0].append(early)
-        ret, last_pair = incoming_carry(own, True, fillers)
+        enters, last_pair = incoming_carry(own, True, fillers)
+        for chunk in range(1, hidden // CHUNK):
+            out_g = out_grad(chunk, out_g, [last_pair])
+        ret = enters([out_g[0]])
         if direct and not first:
             early = pair_sum(early_parts, [last_pair])
             early_rows[layer] = reduce_rows(early)
             waiting.append(early)
-        if z_next is not None:
+        if direct and not final:
             z_next = seq_step([z_next[0]], 2, partner(z_next[1], 2), [last_pair])
             waiting.append(z_next[-1])
         steps = hidden // HALF
@@ -1156,19 +1220,11 @@
                 out_fixed(8 * taps, width),
             ],
             scratch=[pltpu.VMEM((width, 6 * hidden), BF), pltpu.VMEM((2, group, width), F32)]
-            + [extended, pltpu.VMEM((group, width), F32)]
-            + (order if first else []),
+            + [extended, pltpu.VMEM((group, width), F32)],
             flops=in_flops,
             name="conv_back",
         )
         grad, send, sums = res
-        if z_next is not None:
-            dist = 2
-            while len(z_next) == 2:
-                got = partner(z_next[1], 2 * dist)
-                dist *= 2
-                z_next = seq_step([z_next[0]], dist, got, [grad])
-            early_rows[layer + 1] = z_next[0][0]
         if direct and not first:
             late_rows[layer] = reduce_rows(pair_sum(late_parts, [grad]))
         if not direct:
@@ -1181,29 +1237,26 @@
         got = shift(send, -1)
         if first:
             grad = grad.at[:, group - taps + 1 :].add(norm_back(got * first_gain[layer], last_rows))
-        smalls[layer] = jnp.concatenate(
-            [
-                jnp.sum(sums.reshape(taps, 8, width), 1),
-                jnp.sum(sec, 0, keepdims=True),
-                jnp.sum(bias_sum, 0).reshape(-1, width),
-            ],
-            0,
-        )
+        smalls[layer] = (sums, sec, bias_sum)
 
     if direct:
         down_k = down_plan.depth * down_plan.lanes // 128
         up_k = up_plan.depth * up_plan.lanes // 128
         out_k = out_plan.depth * out_plan.lanes // 128
-        done = early_rows[1:]
-        early = reduce_seq(halved, [sums])
+        above = seq_step([z_next[0]], 4, partner(z_next[1], 4), [sums])[0][0]
+        halved = seq_step([halved[0]], 2, partner(halved[1], 2), [sums])
+        packed = pack_small(smalls, taps, [])
+        early = seq_step([halved[0]], 4, partner(halved[1], 4))[0][0]
         late = reduce_seq(seq_step([late_rows[0]], 1))
-        done.insert(0, jnp.concatenate([early, late], 0))
+        done = [jnp.concatenate([early, late], 0), above]
         for layer in range(layers):
             parts = jnp.split(done[layer], [down_k, down_k + up_k, down_k + up_k + out_k])
             plans = (down_plan, up_plan, out_plan, in_plan)
             shards[layer] = tuple(plan.whole(part) for plan, part in zip(plans, parts))[::-1]
+    else:
+        packed = pack_small(smalls, taps, [])
     in_grad, out_grad, up_grad, down_grad = (jnp.stack([s[k] for s in shards]) for k in range(4))
-    every = butterfly(jnp.stack(smalls))
+    every = butterfly(packed)
     sums = every[:, :taps]
     first_grad = jnp.sum(sums * taps_rows, 1)
     taps_grad = (sums * first_gain[:, None]).swapaxes(1, 2)

time: 555 us -> 556 us (level)
  waiting for transfers between devices: 60.2 us -> 50.7 us
  Pallas kernels: 380 us -> 389 us
    ppermute x12, waiting for transfers between devices: 31.9 us -> 22 us  [shift(): return lax.ppermute(block, 'seq', route)]
    pallas_call x31 -> x36, Pallas kernels: 380 us -> 389 us  [call(): pl.pallas_call(kernel, grid=(grid,), in_specs=[s for _, s in ins], out_sp...]
    unnamed x107 -> x95, local copies, waits for them, and re-layouts: 23.5 us -> 19.2 us
  transfers between devices with their start and end apart: 39 -> 39, of which waited for: 23 -> 19; matrix products, arithmetic and copies ran while one was open for 2% -> 2% of each run, Pallas kernels for 35% -> 37%
where the time goes in v2:
time: 556 us; the launch traced here: 550 us
  Pallas kernels  389 us (70%)
  starting transfers between devices  61.5 us (11%)
  waiting for transfers between devices  50.7 us (9%)
  local copies, waits for them, and re-layouts  24.9 us (4%)
  between operations  15.1 us (3%)
  other arithmetic  8.37 us (2%)
    pallas_call x36, Pallas kernels, call(): pl.pallas_call(kernel, grid=(grid,), in_specs=[s for _, s in ins], out_sp...  389 us
    ppermute x12, starting transfers between devices, shift(): return lax.ppermute(block, 'seq', route)  31.2 us
    ppermute x18, waiting for transfers between devices, partner(): lax.ppermute(block, 'seq', [(i, i ^ flip) for i in range(lax.axis_size('s...  23.2 us
    ppermute x12, waiting for transfers between devices, shift(): return lax.ppermute(block, 'seq', route)  22 us
    ppermute x18, starting transfers between devices, partner(): lax.ppermute(block, 'seq', [(i, i ^ flip) for i in range(lax.axis_size('s...  21.6 us
    unnamed x95, local copies, waits for them, and re-layouts  19.2 us
  transfers between devices with their start and end apart: 39, of which 19 were waited for; matrix products, arithmetic and copies ran while one was open for 2% of the time, Pallas kernels for 37%

profile of v2, /device:TPU:0, one launch (start us, length us, event | category | flops | bytes accessed | tf_op | source)
XLA Modules:
  0.0 549.9 jit_solution(3890711900025686374)
XLA Ops:
  8.8 2.3 collective-permute-start
  14.6 22.6 %gates.2 = (f32[6,256,1024]{2,1,0:T(8,128)}, f32[6,256,1024]{2,1,0:T(8,128)}, f32[6,16,1024]{2,1,0:T(8,128)}, f32[2,6,1024]{2,1,0:T(8,128)S(1)}, bf16[512,1536]{...) custom-call(f32[6,256,512]{2,1,0:T(8,128)} %bitcast.150, ...), custom_call_target="tpu_custom_call" | custom-call | flops 9663676416 | bytes 39346176 | tf_op jit(solution)/shard_map/gates/pallas_call | solution.py:701
  37.2 2.8 collective-permute-start.1
  40.9 3.6 collective-permute-start.2
  44.5 1.9 collective-permute-done.2
  46.4 5.6 %collective-permute-start.3 = (f32[2,6,1024]{2,1,0:T(8,128)S(1)}, f32[2,6,1024]{2,1,0:T(8,128)S(1)}, u32[]{:S(2)}, u32[]{:S(2)}) collective-permute-start(f32[2,6,1024]{2,1,0:T(8,128)S(1)} %pad_maximum_fusion.8), channel_id=1, source_target_pairs={{0,4},{1,5},{2,6},{3,7},{8,12},{9,13},{10,14},{11,15},{16,20},{17,... | collective-permute-start | bytes 147464 | tf_op jit(solution)/shard_map/ppermute | solution.py:724
  54.3 38.9 %ffn.2 = (f32[6,256,512]{2,1,0:T(8,128)}, f32[6,3,512]{2,1,0:T(4,128)}, f32[6,256,512]{2,1,0:T(8,128)}, bf16[1536,1024]{1,0:T(8,128)(2,1)}, bf16[1536,1024]{1,0:...) custom-call(f32[6,256,512]{2,1,0:T(8,128)} %get-tuple-element.112.refs_0_.refs_6_, ...), custom_call_target="tpu_custom_call" | custom-call | flops 24159191040 | bytes 65519616 | tf_op jit(solution)/shard_map/ffn/pallas_call | solution.py:701
  95.5 21.1 %gates.3 = (f32[6,256,1024]{2,1,0:T(8,128)}, f32[6,256,1024]{2,1,0:T(8,128)}, f32[6,16,1024]{2,1,0:T(8,128)}, f32[2,6,1024]{2,1,0:T(8,128)S(1)}, bf16[512,1536]{1,0:T(8,128)(2,1)}, /*index=5*/bf16[512,1536]{1,0:T(8,128)(2,1)}) custom-call(f32[6,256,512]{2,1,0:T(8,128)} %get-tuple-element.117.refs_0_.refs_5_, ...), custom_call_target="tpu_custom_call" | custom-call | flops 9663676416 | bytes 36200448 | tf_op jit(solution)/shard_map/gates/pallas_call | solution.py:701
  116.7 3.2 collective-permute-start.5
  120.8 4.4 collective-permute-start.6
  125.2 1.9 collective-permute-done.6
  127.1 5.7 %collective-permute-start.7 = (f32[2,6,1024]{2,1,0:T(8,128)S(1)}, f32[2,6,1024]{2,1,0:T(8,128)S(1)}, u32[]{:S(2)}, u32[]{:S(2)}) collective-permute-start(f32[2,6,1024]{2,1,0:T(8,128)S(1)} %pad_maximum_fusion.9), channel_id=1, source_target_pairs={{0,4},{1,5},{2,6},{3,7},{8,12},{9,13},{10,14},{11,15},{16,20},{17,... | collective-permute-start | bytes 147464 | tf_op jit(solution)/shard_map/ppermute | solution.py:724
  135.2 39.5 %ffn.3 = (f32[6,256,512]{2,1,0:T(8,128)}, f32[6,3,512]{2,1,0:T(4,128)}, f32[6,256,512]{2,1,0:T(8,128)}, bf16[1536,1024]{1,0:T(8,128)(2,1)}, bf16[1536,1024]{1,0:...) custom-call(f32[6,256,512]{2,1,0:T(8,128)} %get-tuple-element.117.refs_0_.refs_5_, ...), custom_call_target="tpu_custom_call" | custom-call | flops 24159191040 | bytes 65519616 | tf_op jit(solution)/shard_map/ffn/pallas_call | solution.py:701
  175.3 53.4 %ffn_back.2 = (f32[6,256,512]{2,1,0:T(8,128)}, f32[8,512]{1,0:T(8,128)}, f32[4,4,2,128,128]{4,3,2,1,0:T(8,128)}, f32[4,4,2,128,128]{4,3,2,1,0:T(8,128)}, f32[4,4...) custom-call(s32[1]{0:T(128)} %bitcast.15.refs_0_.refs_1_, f32[6,256,512]{2,1,0:T(8,128)} %bitcast.157, ...), custom_call_target="tpu_custom_call" | custom-call | flops 38654705664 | bytes 50429956 | tf_op jit(solution)/shard_map/ffn_back/pallas_call | solution.py:701
  229.2 11.8 %out_back.2 = (f32[6,256,1024]{2,1,0:T(8,128)}, f32[6,16,1024]{2,1,0:T(8,128)}, f32[2,6,1024]{2,1,0:T(8,128)S(1)}, bf16[512,1536]{1,0:T(8,128)(2,1)}, bf16[512,1536]{1,0:T(8,128)(2,1)}) custom-call(f32[6,256,512]{2,1,0:T(8,128)} %get-tuple-element.128.refs_0_.refs_7_, f32[6,256,8]{2,1,0:T(8,128)S(1)} %copy-done.13, ...), custom_call_target="tpu_custom_call" | custom-call | flops 4831838208 | bytes 23560192 | tf_op jit(solution)/shard_map/out_back/pallas_call | solution.py:701
  243.6 6.6 %out_grad.4 = (f32[4,4,1,128,128]{4,3,2,1,0:T(8,128)}, f32[4,4,1,128,128]{4,3,2,1,0:T(8,128)}) custom-call(s32[1]{0:T(128)} %bitcast.15.refs_0_.refs_1_, bf16[512,1536]{1,0:T(8,128)(2,1)} %get-tuple-element.129.refs_1_.refs_2_, bf16[512,1536]{1,0:T(8,128)(2,1)} %get-tuple-element.130.refs_2_.refs_3_, ...), custom_call_target="tpu_custom_call" | custom-call | flops 2415919104 | bytes 11534340 | tf_op jit(solution)/shard_map/out_grad/pallas_call | solution.py:701
  250.9 2.5 neighbour_sum.4.refs_0_
  253.5 2.0 copy-done.1
  257.5 6.5 %out_grad.5 = (f32[4,4,1,128,128]{4,3,2,1,0:T(8,128)}, f32[4,4,1,128,128]{4,3,2,1,0:T(8,128)}) custom-call(f32[2,6,1024]{2,1,0:T(8,128)} %copy-done.15, s32[1]{0:T(128)} %bitcast.15.refs_0_.refs_1_, bf16[512,1536]{1,0:T(8,128)(2,1)} %get-tuple-element.129.refs_1_.refs_2_, ...), custom_call_target="tpu_custom_call", output_to_operand_aliasing={{0}: (6, {}), {1}: (7, {})} | custom-call | flops 2415919104 | bytes 13680644 | tf_op jit(solution)/shard_map/out_grad/pallas_call | solution.py:701
  264.1 23.7 %gates_back.2 = (bf16[1536,1024]{1,0:T(8,128)(2,1)}, bf16[1536,1024]{1,0:T(8,128)(2,1)}, bf16[1536,1024]{1,0:T(8,128)(2,1)}, bf16[1536,1024]{1,0:T(8,128)(2,1)},...) custom-call(f32[4,4,512,128]{3,2,1,0:T(8,128)} %copy-done.1, ...), custom_call_target="tpu_custom_call" | custom-call | flops 9663676416 | bytes 49807364 | tf_op jit(solution)/shard_map/gates_back/pallas_call | solution.py:701
  288.5 18.6 %conv_back.2 = (f32[6,256,512]{2,1,0:T(8,128)}, f32[6,3,512]{2,1,0:T(4,128)S(1)}, f32[32,512]{1,0:T(8,128)S(1)}) custom-call(bf16[1536,1024]{1,0:T(8,128)(2,1)} %get-tuple-element.145.refs_0_, bf16[1536,1024]{1,0:T(8,128)(2,1)} %get-tuple-element.146.refs_1_, bf16[1536,1024]{1,0:T(8,128)(2,1)} %get-tuple-element.147.refs_2_, ...), custom_call_target="tpu_custom_call" | custom-call | flops 9663676416 | bytes 30609408 | tf_op jit(solution)/shard_map/conv_back/pallas_call | solution.py:701
  307.1 2.2 neighbour_sum.5
  313.1 53.8 %ffn_back.3 = (f32[6,256,512]{2,1,0:T(8,128)}, f32[8,512]{1,0:T(8,128)}, f32[4,4,2,128,128]{4,3,2,1,0:T(8,128)}, f32[4,4,2,128,128]{4,3,2,1,0:T(8,128)}, f32[4,4...) custom-call(f32[4,512,128]{2,1,0:T(8,128)} %bitcast.131, s32[1]{0:T(128)} %bitcast.15.refs_0_.refs_1_, ...), custom_call_target="tpu_custom_call" | custom-call | flops 38654705664 | bytes 51478532 | tf_op jit(solution)/shard_map/ffn_back/pallas_call | solution.py:701
  367.0 3.1 collective-permute-start.16
  370.1 2.9 seq_sum.9
  373.1 11.9 %out_back.3 = (f32[6,256,1024]{2,1,0:T(8,128)}, f32[6,16,1024]{2,1,0:T(8,128)}, f32[2,6,1024]{2,1,0:T(8,128)S(1)}, bf16[512,1536]{1,0:T(8,128)(2,1)}, bf16[512,1536]{1,0:T(8,128)(2,1)}) custom-call(f32[2,896,128]{2,1,0:T(8,128)} %get-tuple-element.159.refs_0_, f32[6,256,512]{2,1,0:T(8,128)} %get-tuple-element.155.refs_0_.refs_1_.refs_8_, ...), custom_call_target="tpu_custom_call" | custom-call | flops 4831838208 | bytes 24477696 | tf_op jit(solution)/shard_map/out_back/pallas_call | solution.py:701
  385.0 2.5 neighbour_sum.6.refs_0_
  387.5 2.0 copy-done
  390.7 2.4 collective-permute-start.20
  395.7 7.2 %out_grad.6 = (f32[4,4,1,128,128]{4,3,2,1,0:T(8,128)}, f32[4,4,1,128,128]{4,3,2,1,0:T(8,128)}) custom-call(s32[1]{0:T(128)} %bitcast.15.refs_0_.refs_1_, bf16[512,1536]{1,0:T(8,128)(2,1)} %get-tuple-element.160.refs_1_.refs_2_, bf16[512,1536]{1,0:T(8,128)(2,1)} %get-tuple-element.161.refs_2_.refs_3_, ...), custom_call_target="tpu_custom_call" | custom-call | flops 2415919104 | bytes 11534340 | tf_op jit(solution)/shard_map/out_grad/pallas_call | solution.py:701
  402.9 12.6 %collective-permute-done.19.refs_2_ = f32[2,6,1024]{2,1,0:T(8,128)S(1)} collective-permute-done((f32[2,6,1024]{2,1,0:T(8,128)S(1)}, f32[2,6,1024]{2,1,0:T(8,128)S(1)}, u32[]{:S(2)}, u32[]{:S(2)}) %collective-permute-start.19) | collective-permute-done | bytes 49184 | tf_op jit(solution)/shard_map/ppermute | solution.py:724
  416.8 6.6 %out_grad.7 = (f32[4,4,1,128,128]{4,3,2,1,0:T(8,128)}, f32[4,4,1,128,128]{4,3,2,1,0:T(8,128)}) custom-call(f32[2,6,1024]{2,1,0:T(8,128)} %copy-done.17, s32[1]{0:T(128)} %bitcast.15.refs_0_.refs_1_, bf16[512,1536]{1,0:T(8,128)(2,1)} %get-tuple-element.160.refs_1_.refs_2_, ...), custom_call_target="tpu_custom_call", output_to_operand_aliasing={{0}: (6, {}), {1}: (7, {})} | custom-call | flops 2415919104 | bytes 13680644 | tf_op jit(solution)/shard_map/out_grad/pallas_call | solution.py:701
  424.3 2.5 seq_sum.10
  426.9 23.6 %gates_back.3 = (bf16[1536,1024]{1,0:T(8,128)(2,1)}, bf16[1536,1024]{1,0:T(8,128)(2,1)}, bf16[1536,1024]{1,0:T(8,128)(2,1)}, bf16[1536,1024]{1,0:T(8,128)(2,1)},...) custom-call(f32[1,896,128]{2,1,0:T(8,128)} %get-tuple-element.172.refs_0_, ...), custom_call_target="tpu_custom_call" | custom-call | flops 9663676416 | bytes 46071812 | tf_op jit(solution)/shard_map/gates_back/pallas_call | solution.py:701
  451.7 2.3 seq_sum.11
  454.0 2.8 collective-permute-done.22.refs_2_
  458.6 2.2 neighbour_sum.7.refs_0_
  463.5 3.4 collective-permute-start.32
  467.0 19.6 %conv_back.3 = (f32[6,256,512]{2,1,0:T(8,128)}, f32[6,3,512]{2,1,0:T(4,128)S(1)}, f32[32,512]{1,0:T(8,128)S(1)}) custom-call(f32[4,4,384,128]{3,2,1,0:T(8,128)} %copy-done.4, bf16[1536,1024]{1,0:T(8,128)(2,1)} %get-tuple-element.183.refs_1_, bf16[1536,1024]{1,0:T(8,128)(2,1)} %get-tuple-element.184.refs_2_, bf16[1536,1024]{1,0:T(8,128)(2,1)} %get-tuple-element.185.refs_3_, ...), custom_call_target="tpu_custom_call" | custom-call | flops 9663676416 | bytes 33755136 | tf_op jit(solution)/shard_map/conv_back/pallas_call | solution.py:701
  487.5 2.0 seq_sum.15
  491.9 2.8 collective-permute-start.26
  497.3 2.8 collective-permute-start.27
  503.6 3.2 collective-permute-done.28
  512.9 2.7 collective-permute-start.34
  515.6 2.1 seq_sum.12
  520.4 4.5 collective-permute-done.34.refs_2_
  524.9 4.0 collective-permute-done.30.refs_2_
  533.6 7.5 %collective-permute-done.31.refs_2_ = f32[1,384,128]{2,1,0:T(8,128)S(1)} collective-permute-done((f32[1,384,128]{2,1,0:T(8,128)S(1)}, f32[1,384,128]{2,1,0:T(8,128)S(1)}, u32[]{:S(2)}, u32[]{:S(2)}) %collective-permute-start.31) | collective-permute-done | bytes 196640 | tf_op jit(solution)/shard_map/ppermute | solution.py:728
  (218 shorter events, 60.9 us)
Async XLA Ops:
  7.2 305.3 %reduce-scatter.13.cloned.1.call-start = ((), (), s32[]{:S(2)}) async-start(), calls=%async_computation.4 | async-start | bytes 5242880
  8.8 4.4 collective-permute-start
  12.4 24.8 %copy-start.11 = (f32[6,256,8]{2,1,0:T(8,128)}, f32[6,256,8]{2,1,0:T(8,128)S(1)}, u32[]{:S(2)}) copy-start(f32[6,256,8]{2,1,0:T(8,128)S(1)} %fusion.refs_2_.refs_1_.refs_7_.refs_4_.refs_5_) | copy-start | bytes 147460
  13.2 24.0 %copy-start.31 = (f32[6,3,512]{2,1,0:T(4,128)}, f32[6,3,512]{2,1,0:T(4,128)S(1)}, u32[]{:S(2)}) copy-start(f32[6,3,512]{2,1,0:T(4,128)S(1)} %collective-permute-done.refs_1_.refs_7_) | copy-start | bytes 110596
  37.2 3.7 collective-permute-start.1
  40.9 5.5 collective-permute-start.2
  46.4 7.2 %collective-permute-start.3 = (f32[2,6,1024]{2,1,0:T(8,128)S(1)}, f32[2,6,1024]{2,1,0:T(8,128)S(1)}, u32[]{:S(2)}, u32[]{:S(2)}) collective-permute-start(f32[2,6,1024]{2,1,0:T(8,128)S(1)} %pad_maximum_fusion.8), channel_id=1, source_target_pairs={{0,4},{1,5},{2,6},{3,7},{8,12},{9,13},{10,14},{11,15},{16,20},{17,... | collective-permute-start | bytes 147464 | tf_op jit(solution)/shard_map/ppermute | solution.py:724
  54.3 41.3 %copy-start.12 = (f32[6,256,8]{2,1,0:T(8,128)S(1)}, f32[6,256,8]{2,1,0:T(8,128)}, u32[]{:S(2)}) copy-start(f32[6,256,8]{2,1,0:T(8,128)} %copy-done.11) | copy-start | bytes 147460
  54.3 41.3 %copy-start.26 = (f32[2,512]{1,0:T(2,128)S(1)}, f32[2,512]{1,0:T(2,128)}, u32[]{:S(2)}) copy-start(f32[2,512]{1,0:T(2,128)} %refs_10_.5) | copy-start | bytes 12292
  93.2 2.4 collective-permute-start.4
  116.7 4.1 collective-permute-start.5
  120.8 6.3 %collective-permute-start.6 = (f32[2,6,1024]{2,1,0:T(8,128)S(1)}, f32[2,6,1024]{2,1,0:T(8,128)S(1)}, u32[]{:S(2)}, u32[]{:S(2)}) collective-permute-start(f32[2,6,1024]{2,1,0:T(8,128)S(1)} %fusion.1), channel_id=1, source_target_pairs={{0,2},{1,3},{2,4},{3,5},{4,6},{5,7},{8,10},{9,11},{10,12},{11,13},... | collective-permute-start | bytes 147464 | tf_op jit(solution)/shard_map/ppermute | solution.py:724
  127.1 7.4 %collective-permute-start.7 = (f32[2,6,1024]{2,1,0:T(8,128)S(1)}, f32[2,6,1024]{2,1,0:T(8,128)S(1)}, u32[]{:S(2)}, u32[]{:S(2)}) collective-permute-start(f32[2,6,1024]{2,1,0:T(8,128)S(1)} %pad_maximum_fusion.9), channel_id=1, source_target_pairs={{0,4},{1,5},{2,6},{3,7},{8,12},{9,13},{10,14},{11,15},{16,20},{17,... | collective-permute-start | bytes 147464 | tf_op jit(solution)/shard_map/ppermute | solution.py:724
  175.3 54.0 %copy-start.13 = (f32[6,256,8]{2,1,0:T(8,128)S(1)}, f32[6,256,8]{2,1,0:T(8,128)}, u32[]{:S(2)}) copy-start(f32[6,256,8]{2,1,0:T(8,128)} %copy-done.11) | copy-start | bytes 147460
  228.7 22.2 %collective-permute-start.10 = (f32[4,4,256,128]{3,2,1,0:T(8,128)}, f32[4,4,256,128]{3,2,1,0:T(8,128)S(1)}, u32[]{:S(2)}, u32[]{:S(2)}) collective-permute-start(f32[4,4,256,128]{3,2,1,0:T(8,128)} %bitcast.161), channel_id=1, source_target_pairs={{0,1},{1,0},{2,3},{3,2},{4,5},{5,4},{6,7},{7,6},{8,9},{9,8},{10,11... | collective-permute-start | bytes 6291464 | tf_op jit(solution)/shard_map/ppermute | solution.py:728
  228.7 22.2 %collective-permute-start.11 = (f32[4,4,256,128]{3,2,1,0:T(8,128)}, f32[4,4,256,128]{3,2,1,0:T(8,128)}, u32[]{:S(2)}, u32[]{:S(2)}) collective-permute-start(f32[4,4,256,128]{3,2,1,0:T(8,128)} %bitcast.160), channel_id=1, source_target_pairs={{0,1},{1,0},{2,3},{3,2},{4,5},{5,4},{6,7},{7,6},{8,9},{9,8},{10,11... | collective-permute-start | bytes 6291464 | tf_op jit(solution)/shard_map/ppermute | solution.py:728
  241.0 1.3 collective-permute-start.8
  242.3 8.0 %collective-permute-start.9 = (f32[2,6,1024]{2,1,0:T(8,128)S(1)}, f32[2,6,1024]{2,1,0:T(8,128)S(1)}, u32[]{:S(2)}, u32[]{:S(2)}) collective-permute-start(f32[2,6,1024]{2,1,0:T(8,128)S(1)} %carry.6.refs_3_), channel_id=1, source_target_pairs={{2,0},{3,1},{4,2},{5,3},{6,4},{7,5},{10,8},{11,9},{12,10},{13,11},... | collective-permute-start | bytes 147464 | tf_op jit(solution)/shard_map/ppermute | solution.py:724
  255.4 114.7 %reduce-scatter.15.cloned.1.call-start = ((), (), s32[]{:S(2)}) async-start(), calls=%async_computation.5 | async-start | bytes 3932160
  256.2 7.8 %collective-permute-start.12 = (f32[2,6,1024]{2,1,0:T(8,128)S(1)}, f32[2,6,1024]{2,1,0:T(8,128)S(1)}, u32[]{:S(2)}, u32[]{:S(2)}) collective-permute-start(f32[2,6,1024]{2,1,0:T(8,128)S(1)} %copy-done.16), channel_id=1, source_target_pairs={{4,0},{5,1},{6,2},{7,3},{12,8},{13,9},{14,10},{15,11},{20,16},{21,... | collective-permute-start | bytes 147464 | tf_op jit(solution)/shard_map/ppermute | solution.py:724
  264.1 24.0 %copy-start.34 = (f32[4,4,1,128,128]{4,3,2,1,0:T(8,128)S(1)}, f32[4,4,1,128,128]{4,3,2,1,0:T(8,128)}, u32[]{:S(2)}) copy-start(f32[4,4,1,128,128]{4,3,2,1,0:T(8,128)} %get-tuple-element.156) | copy-start | bytes 3145732
  264.1 24.3 %copy-start.27 = (f32[2,512]{1,0:T(2,128)S(1)}, f32[2,512]{1,0:T(2,128)}, u32[]{:S(2)}) copy-start(f32[2,512]{1,0:T(2,128)} %refs_10_.5) | copy-start | bytes 12292
  287.9 19.2 %collective-permute-start.15 = (f32[4,4,256,128]{3,2,1,0:T(8,128)}, f32[4,4,256,128]{3,2,1,0:T(8,128)S(1)}, u32[]{:S(2)}, u32[]{:S(2)}) collective-permute-start(f32[4,4,256,128]{3,2,1,0:T(8,128)} %bitcast.163), channel_id=1, source_target_pairs={{0,1},{1,0},{2,3},{3,2},{4,5},{5,4},{6,7},{7,6},{8,9},{9,8},{10,11... | collective-permute-start | bytes 6291464 | tf_op jit(solution)/shard_map/ppermute | solution.py:728
  288.2 18.9 %collective-permute-start.14 = (f32[4,4,128,128]{3,2,1,0:T(8,128)S(1)}, f32[4,4,128,128]{3,2,1,0:T(8,128)S(1)}, u32[]{:S(2)}, u32[]{:S(2)}) collective-permute-start(f32[4,4,128,128]{3,2,1,0:T(8,128)S(1)} %bitcast.133), channel_id=1, source_target_pairs={{0,1},{1,0},{2,3},{3,2},{4,5},{5,4},{6,7},{7,6},{8,9},{9,8},{10,11... | collective-permute-start | bytes 3145736 | tf_op jit(solution)/shard_map/ppermute | solution.py:728
  309.3 142.3 %reduce-scatter.17.cloned.1.call-start = ((), (), s32[]{:S(2)}) async-start(), calls=%async_computation.6 | async-start | bytes 5242880
  309.4 3.1 collective-permute-start.13
  367.0 18.0 %collective-permute-start.16 = (f32[4,4,256,128]{3,2,1,0:T(8,128)}, f32[4,4,256,128]{3,2,1,0:T(8,128)S(1)}, u32[]{:S(2)}, u32[]{:S(2)}) collective-permute-start(f32[4,4,256,128]{3,2,1,0:T(8,128)} %bitcast.159), channel_id=1, source_target_pairs={{0,1},{1,0},{2,3},{3,2},{4,5},{5,4},{6,7},{7,6},{8,9},{9,8},{10,11... | collective-permute-start | bytes 6291464 | tf_op jit(solution)/shard_map/ppermute | solution.py:728
  370.0 14.9 %collective-permute-start.17 = (f32[4,4,256,128]{3,2,1,0:T(8,128)}, f32[4,4,256,128]{3,2,1,0:T(8,128)}, u32[]{:S(2)}, u32[]{:S(2)}) collective-permute-start(f32[4,4,256,128]{3,2,1,0:T(8,128)} %bitcast.158), channel_id=1, source_target_pairs={{0,1},{1,0},{2,3},{3,2},{4,5},{5,4},{6,7},{7,6},{8,9},{9,8},{10,11... | collective-permute-start | bytes 6291464 | tf_op jit(solution)/shard_map/ppermute | solution.py:728
  389.5 126.1 %reduce-scatter.19.cloned.1.call-start = ((), (), s32[]{:S(2)}) async-start(), calls=%async_computation.7 | async-start | bytes 3932160
  390.7 32.7 %collective-permute-start.20 = (f32[2,896,128]{2,1,0:T(8,128)S(1)}, f32[2,896,128]{2,1,0:T(8,128)S(1)}, u32[]{:S(2)}, u32[]{:S(2)}) collective-permute-start(f32[2,896,128]{2,1,0:T(8,128)S(1)} %copy-done.42), channel_id=1, source_target_pairs={{0,2},{1,3},{2,0},{3,1},{4,6},{5,7},{6,4},{7,5},{8,10},{9,11},{10,... | collective-permute-start | bytes 2752520 | tf_op jit(solution)/shard_map/ppermute | solution.py:728
  393.1 1.3 collective-permute-start.18
  394.4 21.1 %collective-permute-start.19 = (f32[2,6,1024]{2,1,0:T(8,128)S(1)}, f32[2,6,1024]{2,1,0:T(8,128)S(1)}, u32[]{:S(2)}, u32[]{:S(2)}) collective-permute-start(f32[2,6,1024]{2,1,0:T(8,128)S(1)} %carry.9.refs_3_), channel_id=1, source_target_pairs={{2,0},{3,1},{4,2},{5,3},{6,4},{7,5},{10,8},{11,9},{12,10},{13,11},... | collective-permute-start | bytes 147464 | tf_op jit(solution)/shard_map/ppermute | solution.py:724
  415.5 11.3 %collective-permute-start.21 = (f32[2,6,1024]{2,1,0:T(8,128)S(1)}, f32[2,6,1024]{2,1,0:T(8,128)S(1)}, u32[]{:S(2)}, u32[]{:S(2)}) collective-permute-start(f32[2,6,1024]{2,1,0:T(8,128)S(1)} %carry.10.refs_0_), channel_id=1, source_target_pairs={{4,0},{5,1},{6,2},{7,3},{12,8},{13,9},{14,10},{15,11},{20,16},{21,... | collective-permute-start | bytes 147464 | tf_op jit(solution)/shard_map/ppermute | solution.py:724
  426.9 30.1 %copy-start.3 = (f32[4,4,1,128,128]{4,3,2,1,0:T(8,128)S(1)}, f32[4,4,1,128,128]{4,3,2,1,0:T(8,128)}, u32[]{:S(2)}) copy-start(f32[4,4,1,128,128]{4,3,2,1,0:T(8,128)} %get-tuple-element.175.refs_0_) | copy-start | bytes 3145732
  451.2 5.9 %collective-permute-start.23 = (f32[4,4,256,128]{3,2,1,0:T(8,128)}, f32[4,4,256,128]{3,2,1,0:T(8,128)S(1)}, u32[]{:S(2)}, u32[]{:S(2)}) collective-permute-start(f32[4,4,256,128]{3,2,1,0:T(8,128)} %bitcast.162), channel_id=1, source_target_pairs={{0,1},{1,0},{2,3},{3,2},{4,5},{5,4},{6,7},{7,6},{8,9},{9,8},{10,11... | collective-permute-start | bytes 6291464 | tf_op jit(solution)/shard_map/ppermute | solution.py:728
  451.2 5.6 %collective-permute-start.22 = (f32[4,4,128,128]{3,2,1,0:T(8,128)}, f32[4,4,128,128]{3,2,1,0:T(8,128)}, u32[]{:S(2)}, u32[]{:S(2)}) collective-permute-start(f32[4,4,128,128]{3,2,1,0:T(8,128)} %bitcast.37), channel_id=1, source_target_pairs={{0,1},{1,0},{2,3},{3,2},{4,5},{5,4},{6,7},{7,6},{8,9},{9,8},{10,11... | collective-permute-start | bytes 3145736 | tf_op jit(solution)/shard_map/ppermute | solution.py:728
  463.5 23.2 %collective-permute-start.32 = (f32[1,896,128]{2,1,0:T(8,128)S(1)}, f32[1,896,128]{2,1,0:T(8,128)S(1)}, u32[]{:S(2)}, u32[]{:S(2)}) collective-permute-start(f32[1,896,128]{2,1,0:T(8,128)S(1)} %copy-done.43), channel_id=1, source_target_pairs={{0,4},{1,5},{2,6},{3,7},{4,0},{5,1},{6,2},{7,3},{8,12},{9,13},{10,... | collective-permute-start | bytes 1376264 | tf_op jit(solution)/shard_map/ppermute | solution.py:728
  466.9 43.9 %collective-permute-start.33 = (f32[2,512,128]{2,1,0:T(8,128)S(1)}, f32[2,512,128]{2,1,0:T(8,128)S(1)}, u32[]{:S(2)}, u32[]{:S(2)}) collective-permute-start(f32[2,512,128]{2,1,0:T(8,128)S(1)} %copy-done.36), channel_id=1, source_target_pairs={{0,2},{1,3},{2,0},{3,1},{4,6},{5,7},{6,4},{7,5},{8,10},{9,11},{10,... | collective-permute-start | bytes 1572872 | tf_op jit(solution)/shard_map/ppermute | solution.py:728
  486.6 5.3 collective-permute-start.25
  487.5 31.6 %copy-start.40 = (f32[2,512,4]{1,2,0:T(4,128)S(1)}, f32[2,512,4]{1,2,0:T(4,128)}, u32[]{:S(2)}) copy-start(f32[2,512,4]{1,2,0:T(4,128)} %param.16) | copy-start | bytes 49156
  490.6 9.6 %collective-permute-start.24 = (f32[6,3,512]{2,1,0:T(4,128)S(1)}, f32[6,3,512]{2,1,0:T(4,128)S(1)}, u32[]{:S(2)}, u32[]{:S(2)}) collective-permute-start(f32[6,3,512]{2,1,0:T(4,128)S(1)} %get-tuple-element.188), channel_id=1, source_target_pairs={{1,0},{2,1},{3,2},{4,3},{5,4},{6,5},{7,6},{9,8},{10,9},{11,10},{12... | collective-permute-start | bytes 110600 | tf_op jit(solution)/shard_map/ppermute | solution.py:724
  491.9 5.4 collective-permute-start.26
  497.3 4.8 collective-permute-start.27
  502.1 4.6 collective-permute-start.28
  506.7 4.1 collective-permute-start.29
  512.9 11.9 %collective-permute-start.34 = (f32[1,512,128]{2,1,0:T(8,128)S(1)}, f32[1,512,128]{2,1,0:T(8,128)S(1)}, u32[]{:S(2)}, u32[]{:S(2)}) collective-permute-start(f32[1,512,128]{2,1,0:T(8,128)S(1)} %get-tuple-element.201), channel_id=1, source_target_pairs={{0,4},{1,5},{2,6},{3,7},{4,0},{5,1},{6,2},{7,3},{8,12},{9,13},{10,... | collective-permute-start | bytes 786440 | tf_op jit(solution)/shard_map/ppermute | solution.py:728
  517.7 11.2 %collective-permute-start.30 = (f32[2,384,128]{2,1,0:T(8,128)}, f32[2,384,128]{2,1,0:T(8,128)S(1)}, u32[]{:S(2)}, u32[]{:S(2)}) collective-permute-start(f32[2,384,128]{2,1,0:T(8,128)} %get-tuple-element.195), channel_id=1, source_target_pairs={{0,2},{1,3},{2,0},{3,1},{4,6},{5,7},{6,4},{7,5},{8,10},{9,11},{10,... | collective-permute-start | bytes 1179656 | tf_op jit(solution)/shard_map/ppermute | solution.py:728
  530.8 10.3 %collective-permute-start.31 = (f32[1,384,128]{2,1,0:T(8,128)S(1)}, f32[1,384,128]{2,1,0:T(8,128)S(1)}, u32[]{:S(2)}, u32[]{:S(2)}) collective-permute-start(f32[1,384,128]{2,1,0:T(8,128)S(1)} %get-tuple-element.197), channel_id=1, source_target_pairs={{0,4},{1,5},{2,6},{3,7},{4,0},{5,1},{6,2},{7,3},{8,12},{9,13},{10,... | collective-permute-start | bytes 589832 | tf_op jit(solution)/shard_map/ppermute | solution.py:728
  (36 other events, 206.5 us)
Sparse Core Ops, SparseCore 0:
  255.6 55.6 reduce-scatter.12
  315.1 43.9 reduce-scatter.14
  389.7 54.2 reduce-scatter.16
  462.6 45.5 reduce-scatter.18
